TPU v7x, 32 devices: a whole 2x2x4 slice. The times are simulated.
32 devices in a mesh: sub: 8 (over z, x), blk: 4 (over y, core).
Axes of the slice: x: 2, y: 2, z: 4, core: 2. Of those that a mesh axis runs over, the one named last changes fastest.
Arguments:
- residual: float32 [8, 8, 375, 256], P('sub', 'blk'), may hold values from -6 to 6
- stiffness: bfloat16 [8, 8, 16, 375, 375], P('sub', 'blk'), may hold values from -0.078125 to 0.078125
- pattern: int32 [8, 8, 16], P('sub', 'blk'), may hold values from 0 to 7
- neumann_inv: bfloat16 [8, 8, 375, 375], P('sub', 'blk'), may hold values from -0.3125 to 0.3125
- dirichlet_inv: bfloat16 [8, 8, 375, 375], P('sub', 'blk'), may hold values from -0.3125 to 0.3125
- basis: bfloat16 [8, 8, 375, 192], P('sub', 'blk'), may hold values from -0.5 to 0.5
- node_ops: float32 [8, 3, 192, 192], P('sub'), as said below
- root_inv: float32 [192, 192], replicated, may hold values from -0.4375 to 0.4375
Outputs:
- preconditioned: float32 [8, 8, 375, 256], P('sub', 'blk')
Inputs may be any that keep to these rules, and one draw needn't show every extreme that they name: node_ops[s, l] equals node_ops[t, l] whenever s // 2**l == t // 2**l: one map for each tree node, held by all of its subdomains.
All inputs are finite; a program needn't handle non-finite values.
Results may differ from a plain program's by a relative error of at most 0.004.
Values may be sent and summed in bfloat16 or wider, within the bound.
No kernel may reach another device: no remote copies, remote signals or barrier semaphores. Data moves between devices by JAX's collectives and lax.ppermute only.
A program may use at most 64 MiB of HBM per device.

v0:
```python
import jax
import jax.numpy as jnp
from jax import lax
from jax.sharding import PartitionSpec as P


def swapped(x, axis, distance):
    return lax.ppermute(x, axis, [(i, i ^ 1 << distance) for i in range(lax.axis_size(axis))])


def passed_along(x, axis, by):
    count = lax.axis_size(axis)
    pairs = [(i, i + by) for i in range(count) if 0 <= i + by < count]
    return lax.ppermute(x, axis, pairs)


def tree_solve(values, maps, root_inv):
    highest = lax.Precision.HIGHEST
    level_values = [values]
    current = values
    for level in range(maps.shape[0]):
        own = jnp.einsum("mk,mr->kr", maps[level], current, precision=highest)
        current = own + swapped(own, "sub", level)
        level_values.append(current)
    field = jnp.dot(root_inv, current, precision=highest)
    for level in reversed(range(maps.shape[0])):
        field = jnp.dot(maps[level], field, precision=highest) + level_values[level]
    return field


def shards(residual, stiffness, pattern, neumann_inv, dirichlet_inv, basis, node_ops, root_inv):
    subs = lax.axis_size("sub")
    here = lax.axis_index("sub")
    per_device = residual.shape[1]
    local_ids = jnp.arange(per_device)
    shared = (local_ids == 0) & (here > 0) | (local_ids == per_device - 1) & (here < subs - 1)
    scale = jnp.where(shared, 0.5, 1.0).astype(jnp.float32)[:, None, None]
    scaled_bf = (residual[0] * scale).astype(jnp.bfloat16)
    local_fix = jnp.einsum(
        "jab,jbr->jar", neumann_inv[0], scaled_bf, preferred_element_type=jnp.float32
    )
    partial_coarse = jnp.einsum(
        "jbm,jbr->mr", basis[0], scaled_bf, preferred_element_type=jnp.float32
    )
    share = lax.psum_scatter(partial_coarse, "blk", scatter_dimension=1, tiled=True)
    field = tree_solve(share, node_ops[0], root_inv)
    coarse_fix = lax.all_gather(field.astype(jnp.bfloat16), "blk", axis=1, tiled=True)
    fix_term = jnp.einsum("jbm,mr->jbr", basis[0], coarse_fix, preferred_element_type=jnp.float32)
    combined = ((local_fix + fix_term) * scale)[None]
    incoming = passed_along(combined[:, -1], "sub", 1)
    first = combined[:, 0] + incoming
    returned = passed_along(first, "sub", -1)
    last = jnp.where(here < subs - 1, returned, combined[:, -1])
    assembled = jnp.concatenate([first[:, None], combined[:, 1:-1], last[:, None]], axis=1)
    assembled_bf = assembled.astype(jnp.bfloat16)
    gathered = lax.all_gather(assembled_bf, "blk", axis=1, tiled=True)
    picked = jnp.take(gathered[0], pattern[0], axis=0)
    coupled = jnp.einsum("jpab,jpbr->jar", stiffness[0], picked, preferred_element_type=jnp.float32)
    correction = jnp.einsum(
        "jab,jbr->jar",
        dirichlet_inv[0],
        coupled.astype(jnp.bfloat16),
        preferred_element_type=jnp.float32,
    )
    result = assembled[0] - jnp.where(shared[:, None, None], 0.0, correction)
    return result[None]


def solution(mesh):
    placed = (
        P("sub", "blk", None, None),
        P("sub", "blk", None, None, None),
        P("sub", "blk", None),
        P("sub", "blk", None, None),
        P("sub", "blk", None, None),
        P("sub", "blk", None, None),
        P("sub", None, None, None),
        P(),
    )
    return jax.shard_map(
        shards, mesh=mesh, in_specs=placed, out_specs=P("sub", "blk", None, None), check_vma=False
    )
```

profile of v0, /device:TPU:0, one launch (start us, length us, event | category | flops | bytes accessed | tf_op | source)
XLA Modules:
  0.0 135.6 jit_solution(13649186375401883061)
XLA Ops:
  6.6 1.6 %convolution_bitcast_fusion.2 = f32[192,256]{1,0:T(8,128)S(1)} fusion(bf16[1,2,375,192]{2,3,1,0:T(8,128)(2,1)} %param.13, f32[1,2,375,256]{3,1,2,0:T(2,128)} %param.8, f32[2]{0:T(128)S(1)} %get-tuple-element.5), kind=kOutput, calls=%fused_computation.13 | convolution fusion | flops 74112000 | bytes 1252616 | tf_op jit(solution)/shard_map/jbm,jbr->mr/dot_general | solution.py:42
  9.1 23.5 %reduce-scatter.4.cloned.1.call-done = f32[64,192]{1,0:T(8,128)} async-done(((f32[256,192]{1,0:T(8,128)}), f32[64,192]{1,0:T(8,128)}) %reduce-scatter.4.cloned.1.call-update) | async-done | bytes 49168
  32.6 1.2 convolution_bitcast_fusion.8
  33.8 1.5 %collective-permute-start = (f32[192,64]{0,1:T(8,128)S(1)}, f32[192,64]{0,1:T(8,128)S(1)}, u32[]{:S(2)}, u32[]{:S(2)}) collective-permute-start(f32[192,64]{0,1:T(8,128)S(1)} %convolution_bitcast_fusion.8), channel_id=1, source_target_pairs={{0,4},{4,0},{8,12},{12,8},{16,20},{20,16},{24,28},{28,24},{1,5},{5... | collective-permute-start | bytes 147464 | tf_op jit(solution)/shard_map/ppermute | solution.py:8
  35.3 2.8 %collective-permute-done = f32[192,64]{0,1:T(8,128)S(1)} collective-permute-done((f32[192,64]{0,1:T(8,128)S(1)}, f32[192,64]{0,1:T(8,128)S(1)}, u32[]{:S(2)}, u32[]{:S(2)}) %collective-permute-start) | collective-permute-done | bytes 49184 | tf_op jit(solution)/shard_map/ppermute | solution.py:8
  38.1 1.1 convolution_bitcast_fusion.7
  39.3 1.6 %collective-permute-start.1 = (f32[192,64]{0,1:T(8,128)S(1)}, f32[192,64]{0,1:T(8,128)S(1)}, u32[]{:S(2)}, u32[]{:S(2)}) collective-permute-start(f32[192,64]{0,1:T(8,128)S(1)} %convolution_bitcast_fusion.7), channel_id=1, source_target_pairs={{0,8},{4,12},{8,0},{12,4},{16,24},{20,28},{24,16},{28,20},{1,9},{5... | collective-permute-start | bytes 147464 | tf_op jit(solution)/shard_map/ppermute | solution.py:8
  40.8 2.8 %collective-permute-done.1 = f32[192,64]{0,1:T(8,128)S(1)} collective-permute-done((f32[192,64]{0,1:T(8,128)S(1)}, f32[192,64]{0,1:T(8,128)S(1)}, u32[]{:S(2)}, u32[]{:S(2)}) %collective-permute-start.1) | collective-permute-done | bytes 49184 | tf_op jit(solution)/shard_map/ppermute | solution.py:8
  44.8 2.5 %collective-permute-start.2 = (f32[192,64]{0,1:T(8,128)S(1)}, f32[192,64]{0,1:T(8,128)S(1)}, u32[]{:S(2)}, u32[]{:S(2)}) collective-permute-start(f32[192,64]{0,1:T(8,128)S(1)} %convolution_bitcast_fusion.6), channel_id=1, source_target_pairs={{0,16},{4,20},{8,24},{12,28},{16,0},{20,4},{24,8},{28,12},{1,17},{... | collective-permute-start | bytes 147464 | tf_op jit(solution)/shard_map/ppermute | solution.py:8
  47.2 2.8 %collective-permute-done.2 = f32[192,64]{0,1:T(8,128)S(1)} collective-permute-done((f32[192,64]{0,1:T(8,128)S(1)}, f32[192,64]{0,1:T(8,128)S(1)}, u32[]{:S(2)}, u32[]{:S(2)}) %collective-permute-start.2) | collective-permute-done | bytes 49184 | tf_op jit(solution)/shard_map/ppermute | solution.py:8
  50.0 1.2 fusion.50
  51.2 1.3 fusion.20
  52.5 1.3 fusion.19
  53.8 1.3 fusion.21
  55.0 5.4 %all_gather.6 = bf16[192,256]{0,1:T(8,128)(2,1)S(1)} all-gather(bf16[192,64]{0,1:T(8,128)(2,1)S(1)} %fusion.21), channel_id=1, replica_groups=mesh['sub'=8,'blk'=4] {'blk'}, dimensions={1}, use_global_device_ids=true | all-gather | bytes 122880 | tf_op jit(solution)/shard_map/all_gather | solution.py:47
  60.4 1.3 convolution_bitcast_fusion.1
  62.7 3.4 %collective-permute-start.3 = (f32[1,375,256]{2,0,1:T(1,128)S(1)}, f32[1,375,256]{2,0,1:T(1,128)S(1)}, u32[]{:S(2)}, u32[]{:S(2)}) collective-permute-start(f32[1,375,256]{2,0,1:T(1,128)S(1)} %bitcast.122), channel_id=1, source_target_pairs={{0,4},{4,8},{8,12},{12,16},{16,20},{20,24},{24,28},{1,5},{5,9},{9,... | collective-permute-start | bytes 1152008 | tf_op jit(solution)/shard_map/ppermute | solution.py:14
  66.1 8.6 %collective-permute-done.3 = f32[1,375,256]{2,0,1:T(1,128)S(1)} collective-permute-done((f32[1,375,256]{2,0,1:T(1,128)S(1)}, f32[1,375,256]{2,0,1:T(1,128)S(1)}, u32[]{:S(2)}, u32[]{:S(2)}) %collective-permute-start.3) | collective-permute-done | bytes 384032 | tf_op jit(solution)/shard_map/ppermute | solution.py:14
  75.2 1.3 collective-permute-start.4
  76.5 11.7 %collective-permute-done.4 = f32[1,375,256]{2,0,1:T(1,128)S(1)} collective-permute-done((f32[1,375,256]{2,0,1:T(1,128)S(1)}, f32[1,375,256]{2,0,1:T(1,128)S(1)}, u32[]{:S(2)}, u32[]{:S(2)}) %collective-permute-start.4) | collective-permute-done | bytes 384032 | tf_op jit(solution)/shard_map/ppermute | solution.py:14
  90.4 20.5 %all-gather.2.cloned.1.call-done = bf16[1,8,375,256]{3,2,0,1:T(8,128)(2,1)} async-done(((bf16[1,2,375,256]{3,2,0,1:T(8,128)(2,1)}), bf16[1,8,375,256]{3,2,0,1:T(8,128)(2,1)}) %all-gather.2.cloned.1.call-update) | async-done | bytes 1536016 | tf_op jit(solution)/shard_map/all_gather | solution.py:56
  110.9 5.0 %gather_fusion = bf16[32,375,256]{2,1,0:T(8,128)(2,1)} fusion(bf16[8,375,256]{2,1,0:T(8,128)(2,1)} %bitcast.117, s32[1024]{0:T(1024)S(1)} %pad_clamp_fusion), kind=kCustom, calls=%fused_computation | custom fusion | bytes 12288128 | tf_op jit(solution)/shard_map/jit(_take)/gather | solution.py:57
  115.9 11.0 %fusion.24 = f32[2,256,375]{1,2,0:T(8,128)S(1)} fusion(bf16[2,375,375]{2,0,1:T(2,128)(2,1)S(1)} %bitcast.124, bf16[2,16,375,375]{3,1,2,0:T(8,128)(2,1)} %bitcast.123, bf16[2,16,375,256]{3,2,1,0:T(8,128)(2,1)} %bitcast.118, pred[2,16]{1,0:T(4,128)(4,1)S(1)} %compare_and_fusion), kind=kOutput, calls=%fused_computation.31 | convolution fusion | flops 2451264000 | bytes 16474532 | tf_op jit(solution)/shard_map/jab,jbr->jar/dot_general | solution.py:59
  126.9 1.8 %fusion.23 = f32[1,2,375,256]{3,1,2,0:T(2,128)} fusion(f32[2,256,375]{1,2,0:T(8,128)S(1)} %fusion.24, pred[2]{0:T(512)(128)(4,1)S(1)} %get-tuple-element.6, f32[1,1,375,256]{3,1,2,0:T(1,128)S(1)} %fusion.31, f32[1,1,375,256]{3,1,2,0:T(1,128)S(1)} %bitcast.120), kind=kLoop, calls=%fused_computation.28 | loop fusion | flops 576000 | bytes 2304002 | tf_op jit(solution)/shard_map/broadcast_in_dim | solution.py:66
  (28 shorter events, 5.6 us)
Async XLA Ops:
  6.5 55.2 %copy-start = (bf16[1,2,375,375]{3,1,2,0:T(2,128)(2,1)S(1)}, bf16[1,2,375,375]{3,1,2,0:T(2,128)(2,1)}, u32[]{:S(2)}) copy-start(bf16[1,2,375,375]{3,1,2,0:T(2,128)(2,1)} %param.11) | copy-start | bytes 1687504
  6.5 55.2 %copy-start.1 = (f32[1,2,375,256]{3,1,2,0:T(2,128)S(1)}, f32[1,2,375,256]{3,1,2,0:T(2,128)}, u32[]{:S(2)}) copy-start(f32[1,2,375,256]{3,1,2,0:T(2,128)} %param.8) | copy-start | bytes 2304004
  6.5 26.0 %reduce-scatter.4.cloned.1.call-start = ((), (), s32[]{:S(2)}) async-start(), calls=%async_computation.2 | async-start | bytes 327680
  9.0 101.8 %all-gather.2.cloned.1.call-start = ((), (), s32[]{:S(2)}) async-start(), calls=%async_computation.1 | async-start | bytes 1925120 | tf_op jit(solution)/shard_map/all_gather | solution.py:56
  33.8 4.3 %collective-permute-start = (f32[192,64]{0,1:T(8,128)S(1)}, f32[192,64]{0,1:T(8,128)S(1)}, u32[]{:S(2)}, u32[]{:S(2)}) collective-permute-start(f32[192,64]{0,1:T(8,128)S(1)} %convolution_bitcast_fusion.8), channel_id=1, source_target_pairs={{0,4},{4,0},{8,12},{12,8},{16,20},{20,16},{24,28},{28,24},{1,5},{5... | collective-permute-start | bytes 147464 | tf_op jit(solution)/shard_map/ppermute | solution.py:8
  39.3 4.3 %collective-permute-start.1 = (f32[192,64]{0,1:T(8,128)S(1)}, f32[192,64]{0,1:T(8,128)S(1)}, u32[]{:S(2)}, u32[]{:S(2)}) collective-permute-start(f32[192,64]{0,1:T(8,128)S(1)} %convolution_bitcast_fusion.7), channel_id=1, source_target_pairs={{0,8},{4,12},{8,0},{12,4},{16,24},{20,28},{24,16},{28,20},{1,9},{5... | collective-permute-start | bytes 147464 | tf_op jit(solution)/shard_map/ppermute | solution.py:8
  44.8 5.2 %collective-permute-start.2 = (f32[192,64]{0,1:T(8,128)S(1)}, f32[192,64]{0,1:T(8,128)S(1)}, u32[]{:S(2)}, u32[]{:S(2)}) collective-permute-start(f32[192,64]{0,1:T(8,128)S(1)} %convolution_bitcast_fusion.6), channel_id=1, source_target_pairs={{0,16},{4,20},{8,24},{12,28},{16,0},{20,4},{24,8},{28,12},{1,17},{... | collective-permute-start | bytes 147464 | tf_op jit(solution)/shard_map/ppermute | solution.py:8
  51.2 39.0 %copy-start.2 = (s32[1,2,16]{2,1,0:T(2,128)S(1)}, s32[1,2,16]{2,1,0:T(2,128)}, u32[]{:S(2)}) copy-start(s32[1,2,16]{2,1,0:T(2,128)} %param.10) | copy-start | bytes 388
  62.7 12.1 %collective-permute-start.3 = (f32[1,375,256]{2,0,1:T(1,128)S(1)}, f32[1,375,256]{2,0,1:T(1,128)S(1)}, u32[]{:S(2)}, u32[]{:S(2)}) collective-permute-start(f32[1,375,256]{2,0,1:T(1,128)S(1)} %bitcast.122), channel_id=1, source_target_pairs={{0,4},{4,8},{8,12},{12,16},{16,20},{20,24},{24,28},{1,5},{5,9},{9,... | collective-permute-start | bytes 1152008 | tf_op jit(solution)/shard_map/ppermute | solution.py:14
  75.2 13.0 %collective-permute-start.4 = (f32[1,375,256]{2,0,1:T(1,128)S(1)}, f32[1,375,256]{2,0,1:T(1,128)S(1)}, u32[]{:S(2)}, u32[]{:S(2)}) collective-permute-start(f32[1,375,256]{2,0,1:T(1,128)S(1)} %fusion.32), channel_id=1, source_target_pairs={{4,0},{8,4},{12,8},{16,12},{20,16},{24,20},{28,24},{5,1},{9,5},{13... | collective-permute-start | bytes 1152008 | tf_op jit(solution)/shard_map/ppermute | solution.py:14
  110.9 5.0 %copy-start.3 = (bf16[1,2,375,375]{3,1,2,0:T(2,128)(2,1)S(1)}, bf16[1,2,375,375]{3,1,2,0:T(2,128)(2,1)}, u32[]{:S(2)}) copy-start(bf16[1,2,375,375]{3,1,2,0:T(2,128)(2,1)} %param.12) | copy-start | bytes 1687504
Sparse Core Ops, SparseCore 0:
  9.8 22.7 reduce-scatter.3
  90.4 20.4 all-gather.1
where the time goes:
time: 136 us
  waiting for transfers between devices  72.7 us (53%)
  matrix products  22.8 us (17%)
  between operations  13.6 us (10%)
  starting transfers between devices  10.3 us (8%)
  local copies, waits for them, and re-layouts  7.19 us (5%)
  blocking collectives  5.42 us (4%)
  other arithmetic  3.6 us (3%)
    unnamed x3, waiting for transfers between devices  23.5 us
    all_gather x1, waiting for transfers between devices, shards(): gathered = lax.all_gather(assembled_bf, 'blk', axis=1, tiled=True)  20.5 us
    ppermute x2, waiting for transfers between devices, passed_along(): return lax.ppermute(x, axis, pairs)  20.3 us
    dot_general x1, matrix products, shards(): jnp.einsum('jab,jbr->jar', dirichlet_inv[0], coupled.astype(jnp.bfloat16)...  11 us
    ppermute x3, waiting for transfers between devices, swapped(): lax.ppermute(x, axis, [(i, i ^ 1 << distance) for i in range(lax.axis_siz...  8.31 us
    ppermute x3, starting transfers between devices, swapped(): lax.ppermute(x, axis, [(i, i ^ 1 << distance) for i in range(lax.axis_siz...  5.58 us
    all_gather x1, blocking collectives, shards(): lax.all_gather(field.astype(jnp.bfloat16), 'blk', axis=1, tiled=True)  5.42 us
    gather x1, local copies, waits for them, and re-layouts, shards(): picked = jnp.take(gathered[0], pattern[0], axis=0)  5.02 us
  transfers between devices with their start and end apart: 7, of which 7 were waited for; matrix products, arithmetic and copies ran while one was open for 0% of the time, Pallas kernels for 0%

commit v1 on v0

v1 whole, which is shorter than its diff:
```python
import functools

import jax
import jax.numpy as jnp
from jax import lax
from jax.experimental import pallas as pl
from jax.experimental.pallas import tpu as pltpu
from jax.sharding import PartitionSpec as P

HIGHEST = lax.Precision.HIGHEST
BF = jnp.bfloat16
F32 = jnp.float32


def route(x, subs, blks, target):
    pairs = []
    for s in range(subs):
        for b in range(blks):
            to = target(s, b)
            if to is not None and 0 <= to[0] < subs and 0 <= to[1] < blks:
                pairs.append((s * blks + b, to[0] * blks + to[1]))
    return lax.ppermute(x, ("sub", "blk"), pairs)


def dot(a, b):
    return jnp.dot(a, b, precision=HIGHEST, preferred_element_type=F32)


def tdot(a, b):
    return lax.dot_general(
        a, b, (((0,), (0,)), ((), ())), precision=HIGHEST, preferred_element_type=F32
    )


def stiffness_kernel(pattern_ref, matrix_ref, values_ref, inverse_ref, out_ref):
    total = jnp.zeros(out_ref.shape, F32)
    for k in range(matrix_ref.shape[0]):
        total += jnp.dot(
            matrix_ref[k], values_ref[pattern_ref[k]], preferred_element_type=F32
        )
    out_ref[...] = jnp.dot(
        inverse_ref[...], total.astype(BF), preferred_element_type=F32
    )


def corrected(columns, matrix, values, inverse):
    coupled, block, _ = matrix.shape
    loads = values.shape[-1]
    vmem = pl.BlockSpec(memory_space=pltpu.VMEM)
    return pl.pallas_call(
        stiffness_kernel,
        out_shape=jax.ShapeDtypeStruct((block, loads), F32),
        in_specs=[pl.BlockSpec(memory_space=pltpu.SMEM), vmem, vmem, vmem],
        out_specs=vmem,
        compiler_params=pltpu.CompilerParams(vmem_limit_bytes=32 * 1024 * 1024),
        cost_estimate=pl.CostEstimate(
            flops=2 * coupled * block * block * loads,
            bytes_accessed=2 * coupled * block * block,
            transcendentals=0,
        ),
    )(columns, matrix, values, inverse)


def shards(subs, blks, residual, stiffness, pattern, neumann_inv, dirichlet_inv, basis, node_ops, root_inv):
    here = lax.axis_index("sub")
    mine = lax.axis_index("blk")
    per = residual.shape[1]
    levels = node_ops.shape[1]
    even = here % 2 == 0
    edge = (here == 0) | (here == subs - 1)
    go = functools.partial(route, subs=subs, blks=blks)

    def lead(f):
        return lambda s, b: f(s, b) if b % 2 == 1 else None

    local_ids = jnp.arange(per)
    shared = (local_ids == 0) & (here > 0) | (local_ids == per - 1) & (here < subs - 1)
    scale = jnp.where(shared, 0.5, 1.0).astype(F32)[:, None, None]
    scaled_bf = (residual[0] * scale).astype(BF)
    modes = basis[0]

    partial = jnp.einsum("jbm,jbr->mr", modes, scaled_bf, preferred_element_type=F32)
    coarse = partial + go(partial, target=lambda s, b: (s, b ^ 1) if b % 2 == 0 else None)
    step = 2
    while step < blks:
        coarse = coarse + go(coarse.astype(BF), target=lead(lambda s, b, k=step: (s, b ^ k))).astype(F32)
        step *= 2

    local_fix = jnp.einsum("jab,jbr->jar", neumann_inv[0], scaled_bf, preferred_element_type=F32)
    local_bf = local_fix.astype(BF)

    first = jnp.concatenate([modes[0], local_bf[0]], axis=1)
    last = jnp.concatenate([modes[-1], local_bf[-1]], axis=1)
    to_sibling = jnp.where(even, last, first)
    to_far = jnp.where(even, first, last)
    far = lambda s, b: (s - 1 if s % 2 == 0 else s + 1, b)
    from_sibling = go(to_sibling, target=lambda s, b: (s ^ 1, b))
    from_far = go(to_far, target=far)

    maps = node_ops[0]
    sibling_map = go(maps[0], target=lead(lambda s, b: (s ^ 1, b)))
    top = root_inv
    for level in reversed(range(1, levels)):
        top = dot(maps[level], top)
    own_top = dot(maps[0], top)
    sibling_top = dot(sibling_map, top)
    across = lead(lambda s, b: (s + 2 if s % 2 == 0 else s - 2, b))
    far_top = go(sibling_top.astype(BF), target=across).astype(F32)

    sibling = go(coarse.astype(BF), target=lead(lambda s, b: (s ^ 1, b))).astype(F32)
    current = tdot(maps[0], coarse) + tdot(sibling_map, sibling)
    values = [coarse, current]
    for level in range(1, levels):
        own = tdot(maps[level], current)
        if level == levels - 1:
            down = current
            for below in reversed(range(1, levels - 1)):
                down = dot(maps[below], down) + values[below]
            own_rest = dot(maps[0], down) + coarse
            sibling_rest = dot(sibling_map, down) + sibling
            far_rest = go(sibling_rest.astype(BF), target=across).astype(F32)
        current = own + go(own.astype(BF), target=lead(lambda s, b, k=2**level: (s ^ k, b))).astype(F32)
        values.append(current)
    fields = jnp.stack(
        [
            dot(own_top, current) + own_rest,
            dot(sibling_top, current) + sibling_rest,
            dot(far_top, current) + far_rest,
        ]
    ).astype(BF)
    sent = go(fields, target=lambda s, b: (s, b ^ 1) if b % 2 == 1 else None)
    fields = jnp.where(mine % 2 == 1, fields, sent)

    def spread(mode_block, field):
        return jnp.dot(mode_block, field, preferred_element_type=F32)

    width = modes.shape[-1]

    def face(received, field):
        return 0.5 * (received[:, width:].astype(F32) + spread(received[:, :width], field))

    combined = [(local_fix[j] + spread(modes[j], fields[0])) * scale[j] for j in range(per)]
    sibling_face = face(from_sibling, fields[1])
    far_face = jnp.where(edge, 0.0, face(from_far, fields[2]))
    assembled = list(combined)
    assembled[0] = combined[0] + jnp.where(even, far_face, sibling_face)
    assembled[-1] = combined[-1] + jnp.where(even, sibling_face, far_face)

    wanted = lambda s: per > 2 or s in (0, subs - 1)
    gathered = jnp.stack(assembled).astype(BF)
    step = blks // 2
    while step:
        more = go(gathered, target=lambda s, b, k=step: (s, b ^ k) if wanted(s) else None)
        gathered = jnp.concatenate([gathered, more])
        step //= 2
    order = [0]
    step = blks // 2
    while step:
        order = order + [d ^ step for d in order]
        step //= 2
    place = jnp.array([order.index(d) for d in range(blks)], jnp.int32)
    columns = place[(pattern[0] // per) ^ mine] * per + pattern[0] % per

    def correction(j):
        return corrected(columns[j], stiffness[0, j], gathered, dirichlet_inv[0, j])

    def picked(x):
        return jnp.where(here == 0, x[0], x[per - 1])

    edge_fix = corrected(
        picked(columns),
        lax.dynamic_index_in_dim(stiffness[0], jnp.where(here == 0, 0, per - 1), 0, False),
        gathered,
        picked(dirichlet_inv[0]),
    )
    result = []
    for j in range(per):
        if 0 < j < per - 1:
            fix = correction(j)
        else:
            fix = jnp.where(shared[j], 0.0, edge_fix)
        result.append(assembled[j] - fix)
    return jnp.stack(result)[None]


def solution(mesh):
    placed = (
        P("sub", "blk", None, None),
        P("sub", "blk", None, None, None),
        P("sub", "blk", None),
        P("sub", "blk", None, None),
        P("sub", "blk", None, None),
        P("sub", "blk", None, None),
        P("sub", None, None, None),
        P(),
    )
    return jax.shard_map(
        functools.partial(shards, mesh.shape["sub"], mesh.shape["blk"]),
        mesh=mesh,
        in_specs=placed,
        out_specs=P("sub", "blk", None, None),
        check_vma=False,
    )
```

time: 136 us -> 84.3 us (0.62)
  waiting for transfers between devices: 72.7 us -> 29.1 us
  between operations: 13.6 us -> 0.52 us
  starting transfers between devices: 10.3 us -> 20.6 us
  matrix products: 22.8 us -> 15.2 us
  blocking collectives: 5.42 us -> 0 us
  Pallas kernels: 0 us -> 2.77 us
  local copies, waits for them, and re-layouts: 7.19 us -> 9.46 us
  other arithmetic: 3.6 us -> 5.86 us
    unnamed x3 -> x0, waiting for transfers between devices: 23.5 us -> none
    all_gather x1 -> x0, waiting for transfers between devices: 20.5 us -> none  [shards(): gathered = lax.all_gather(assembled_bf, 'blk', axis=1, tiled=True)]
    ppermute x5 -> x13, starting transfers between devices: 10.3 us -> 20.6 us  [route(): return lax.ppermute(x, ('sub', 'blk'), pairs)]
    dot_general x10 -> x19, matrix products: 22.4 us -> 14.8 us  [the longest x10 5.68 us: dot(): return jnp.dot(a, b, precision=HIGHEST, preferred_element_type=F32)]
    all_gather x1 -> x0, blocking collectives: 5.42 us -> none  [shards(): lax.all_gather(field.astype(jnp.bfloat16), 'blk', axis=1, tiled=True)]
    gather x1, local copies, waits for them, and re-layouts: 5.02 us -> 0.7 us  [shards(): columns = place[pattern[0] // per ^ mine] * per + pattern[0] % per]
    dynamic_slice x0 -> x2, local copies, waits for them, and re-layouts: none -> 3.8 us  [shards(): lax.dynamic_index_in_dim(stiffness[0], jnp.where(here == 0, 0, per - 1),...]
    pallas_call x0 -> x1, Pallas kernels: none -> 2.77 us  [corrected(): pl.pallas_call(stiffness_kernel, out_shape=jax.ShapeDtypeStruct((block, l...]
  transfers between devices with their start and end apart: 7 -> 13, of which waited for: 7 -> 2; matrix products, arithmetic and copies ran while one was open for 0% -> 22% of each run, Pallas kernels for 0% -> 0%
where the time goes in v1:
time: 84.3 us; the launch traced here: 83.6 us
  waiting for transfers between devices  29.1 us (35%)
  starting transfers between devices  20.6 us (24%)
  matrix products  15.2 us (18%)
  local copies, waits for them, and re-layouts  9.46 us (11%)
  other arithmetic  5.86 us (7%)
  Pallas kernels  2.77 us (3%)
    ppermute x13, waiting for transfers between devices, route(): return lax.ppermute(x, ('sub', 'blk'), pairs)  29.1 us
    ppermute x13, starting transfers between devices, route(): return lax.ppermute(x, ('sub', 'blk'), pairs)  20.6 us
    dot_general x10, matrix products, dot(): return jnp.dot(a, b, precision=HIGHEST, preferred_element_type=F32)  5.68 us
    dot_general x4, matrix products, spread(): return jnp.dot(mode_block, field, preferred_element_type=F32)  5.13 us
    dynamic_slice x2, local copies, waits for them, and re-layouts, shards(): lax.dynamic_index_in_dim(stiffness[0], jnp.where(here == 0, 0, per - 1),...  3.8 us
    pallas_call x1, Pallas kernels, corrected(): pl.pallas_call(stiffness_kernel, out_shape=jax.ShapeDtypeStruct((block, l...  2.77 us
    dot_general x4, matrix products, tdot(): lax.dot_general(a, b, (((0,), (0,)), ((), ())), precision=HIGHEST, prefer...  2.1 us
    dot_general x1, matrix products, shards(): jnp.einsum('jbm,jbr->mr', modes, scaled_bf, preferred_element_type=F32)  1.91 us
  transfers between devices with their start and end apart: 13, of which 2 were waited for; matrix products, arithmetic and copies ran while one was open for 22% of the time, Pallas kernels for 0%

profile of v1, /device:TPU:0, one launch (start us, length us, event | category | flops | bytes accessed | tf_op | source)
XLA Modules:
  0.0 83.6 jit_solution(1938123957000726203)
XLA Ops:
  0.0 1.6 %fusion.14 = bf16[2,375,256]{2,0,1:T(2,128)(2,1)S(1)} fusion(f32[1,2,375,256]{3,1,2,0:T(2,128)} %param.9, f32[2]{0:T(128)S(1)} %get-tuple-element.7), kind=kLoop, calls=%fused_computation.33 | loop fusion | flops 384000 | bytes 1152008 | tf_op jit(solution)/shard_map/convert_element_type | solution.py:79
  1.6 1.9 %convolution_bitcast_fusion.7 = f32[192,256]{1,0:T(8,128)} fusion(bf16[2,375,256]{2,0,1:T(2,128)(2,1)S(1)} %fusion.14, bf16[1,2,375,192]{2,3,1,0:T(8,128)(2,1)} %param.14), kind=kOutput, calls=%fused_computation.23 | convolution fusion | flops 73728000 | bytes 868608 | tf_op jit(solution)/shard_map/jbm,jbr->mr/dot_general | solution.py:82
  3.5 3.0 %collective-permute-start = (f32[192,256]{1,0:T(8,128)}, f32[192,256]{1,0:T(8,128)}, u32[]{:S(2)}, u32[]{:S(2)}) collective-permute-start(f32[192,256]{1,0:T(8,128)} %convolution_bitcast_fusion.7), channel_id=1, source_target_pairs={{0,1},{2,3},{4,5},{6,7},{8,9},{10,11},{12,13},{14,15},{16,17},{18,... | collective-permute-start | bytes 589832 | tf_op jit(solution)/shard_map/ppermute | solution.py:22
  8.7 1.2 %broadcast_select_fusion.1 = (bf16[375,448]{1,0:T(8,128)(2,1)}, bf16[375,448]{1,0:T(8,128)(2,1)}) fusion(pred[]{:T(512)S(6)} %eq.37, bf16[375,256]{1,0:T(8,128)(2,1)S(1)} %get-tuple-element.16, bf16[375,192]{1,0:T(8,128)(2,1)S(1)} %bitcast.153, bf16[375,256]{1,0:T(8,128)(2,1)S(1)} %get-tuple-element.15, bf16[375,192]{1,0:T(8,128)(2,1)S(1)} %bitcast.152), kind=kLoop, calls=%fused_computation.45 | loop fusion | flops 1680000 | bytes 1344001 | tf_op jit(solution)/shard_map/jit(_where)/select_n | solution.py:95
  9.9 0.8 collective-permute-start.9
  10.8 5.2 %collective-permute-start.10 = (bf16[375,448]{1,0:T(8,128)(2,1)}, bf16[375,448]{1,0:T(8,128)(2,1)}, u32[]{:S(2)}, u32[]{:S(2)}) collective-permute-start(bf16[375,448]{1,0:T(8,128)(2,1)} %get-tuple-element.10), channel_id=1, source_target_pairs={{0,4},{1,5},{2,6},{3,7},{4,0},{5,1},{6,2},{7,3},{8,12},{9,13},{10,... | collective-permute-start | bytes 1008008 | tf_op jit(solution)/shard_map/ppermute | solution.py:22
  15.9 1.2 %fusion.25 = f32[192,192]{1,0:T(8,128)S(1)} fusion(f32[192,192]{1,0:T(8,128)} %param.16, f32[1,3,192,192]{3,2,1,0:T(8,128)S(1)} %copy-done.2), kind=kOutput, calls=%fused_computation.58 | convolution fusion | flops 84934656 | bytes 491520 | tf_op jit(solution)/shard_map/dot_general | solution.py:26
  17.9 1.0 %fusion.44 = f32[192,192]{1,0:T(8,128)} fusion(f32[192,192]{1,0:T(8,128)S(1)} %fusion.22, f32[1,3,192,192]{3,2,1,0:T(8,128)S(1)} %copy-done.2), kind=kOutput, calls=%fused_computation.104 | convolution fusion | flops 84934656 | bytes 540672 | tf_op jit(solution)/shard_map/dot_general | solution.py:26
  18.9 1.0 %fusion.45 = (bf16[192,256]{1,0:T(8,128)(2,1)S(1)}, f32[192,256]{1,0:T(8,128)S(1)}) fusion(f32[192,256]{1,0:T(8,128)} %convolution_bitcast_fusion.7, f32[192,256]{1,0:T(8,128)} %collective-permute-done), kind=kLoop, calls=%fused_computation.105 | loop fusion | flops 98304 | bytes 688128 | tf_op jit(solution)/shard_map/convert_element_type | solution.py:86
  25.9 0.8 collective-permute-start.5
  30.0 1.3 %collective-permute-start.8 = (bf16[3,192,256]{2,1,0:T(8,128)(2,1)S(1)}, bf16[3,192,256]{2,1,0:T(8,128)(2,1)S(1)}, u32[]{:S(2)}, u32[]{:S(2)}) collective-permute-start(bf16[3,192,256]{2,1,0:T(8,128)(2,1)S(1)} %pad_maximum_fusion.5), channel_id=1, source_target_pairs={{1,0},{3,2},{5,4},{7,6},{9,8},{11,10},{13,12},{15,14},{17,16},{19,... | collective-permute-start | bytes 884744 | tf_op jit(solution)/shard_map/ppermute | solution.py:22
  32.0 22.5 %collective-permute-done.8 = bf16[3,192,256]{2,1,0:T(8,128)(2,1)S(1)} collective-permute-done((bf16[3,192,256]{2,1,0:T(8,128)(2,1)S(1)}, bf16[3,192,256]{2,1,0:T(8,128)(2,1)S(1)}, u32[]{:S(2)}, u32[]{:S(2)}) %collective-permute-start.8) | collective-permute-done | bytes 294944 | tf_op jit(solution)/shard_map/ppermute | solution.py:22
  54.7 1.1 %fusion.27 = f32[375,256]{1,0:T(8,128)S(1)} fusion(bf16[375,448]{1,0:T(8,128)(2,1)} %collective-permute-done.10, bf16[3,192,256]{2,1,0:T(8,128)(2,1)S(1)} %broadcast_select_fusion.2), kind=kOutput, calls=%fused_computation.64 | convolution fusion | flops 36864000 | bytes 674816 | tf_op jit(solution)/shard_map/dot_general | solution.py:135
  55.9 1.9 %fusion.4 = f32[375,256]{1,0:T(8,128)S(1)} fusion(f32[2,375,256]{2,1,0:T(8,128)S(1)} %get-tuple-element.24, f32[375,256]{1,0:T(8,128)S(1)} %fusion.27, f32[375,256]{1,0:T(8,128)S(1)} %fusion.29, f32[]{:T(128)} %bitcast.36, pred[]{:T(512)S(6)} %or.11, pred[]{:T(512)S(6)} %eq.37, bf16[375,448]{1,0:T(8,128)(2,1)} %collective-permute-done.10, ...), kind=kOutput, calls=%fused_computation.10 | convolution fusion | flops 37920000 | bytes 2169350 | tf_op jit(solution)/shard_map/dot_general | solution.py:135
  57.7 2.0 %fusion.5 = f32[375,256]{1,0:T(8,128)S(1)} fusion(f32[2,375,256]{2,1,0:T(8,128)S(1)} %get-tuple-element.24, f32[375,256]{1,0:T(8,128)S(1)} %fusion.27, f32[375,256]{1,0:T(8,128)S(1)} %fusion.29, f32[]{:T(128)} %bitcast.22, pred[]{:T(512)S(6)} %or.11, pred[]{:T(512)S(6)} %eq.37, bf16[375,448]{1,0:T(8,128)(2,1)} %collective-permute-done.10, ...), kind=kOutput, calls=%fused_computation.11 | convolution fusion | flops 37920000 | bytes 2169350 | tf_op jit(solution)/shard_map/dot_general | solution.py:135
  59.8 3.4 %collective-permute-start.11 = (bf16[2,375,256]{2,1,0:T(8,128)(2,1)S(1)}, bf16[2,375,256]{2,1,0:T(8,128)(2,1)S(1)}, u32[]{:S(2)}, u32[]{:S(2)}) collective-permute-start(bf16[2,375,256]{2,1,0:T(8,128)(2,1)S(1)} %pad_maximum_fusion.4), channel_id=1, source_target_pairs={{0,2},{1,3},{2,0},{3,1},{28,30},{29,31},{30,28},{31,29}} | collective-permute-start | bytes 1152008 | tf_op jit(solution)/shard_map/ppermute | solution.py:22
  63.2 2.8 %constant_dynamic-slice_fusion = bf16[1,1,16,375,375]{4,2,3,1,0:T(8,128)(2,1)S(1)} fusion(bf16[1,2,16,375,375]{4,2,3,1,0:T(8,128)(2,1)} %param.10, s32[]{:T(128)S(6)} %select_n.144), kind=kLoop, calls=%fused_computation.101 | loop fusion | bytes 9000004 | tf_op jit(solution)/shard_map/jit(dynamic_index_in_dim)/dynamic_slice | solution.py:172
  66.0 6.7 %collective-permute-done.11 = bf16[2,375,256]{2,1,0:T(8,128)(2,1)S(1)} collective-permute-done((bf16[2,375,256]{2,1,0:T(8,128)(2,1)S(1)}, bf16[2,375,256]{2,1,0:T(8,128)(2,1)S(1)}, u32[]{:S(2)}, u32[]{:S(2)}) %collective-permute-start.11) | collective-permute-done | bytes 384032 | tf_op jit(solution)/shard_map/ppermute | solution.py:22
  73.1 2.1 %collective-permute-start.12 = (bf16[4,375,256]{2,0,1:T(4,128)(2,1)S(1)}, bf16[4,375,256]{2,0,1:T(4,128)(2,1)S(1)}, u32[]{:S(2)}, u32[]{:S(2)}) collective-permute-start(bf16[4,375,256]{2,0,1:T(4,128)(2,1)S(1)} %copy.34), channel_id=1, source_target_pairs={{0,1},{1,0},{2,3},{3,2},{28,29},{29,28},{30,31},{31,30}} | collective-permute-start | bytes 2304008 | tf_op jit(solution)/shard_map/ppermute | solution.py:22
  75.8 1.0 %copy.58 = bf16[1,1,16,375,375]{4,3,2,1,0:T(8,128)(2,1)S(1)} copy(bf16[1,1,16,375,375]{4,2,3,1,0:T(8,128)(2,1)S(1)} %constant_dynamic-slice_fusion) | data formatting | bytes 9000000 | tf_op jit(solution)/shard_map/jit(dynamic_index_in_dim)/dynamic_slice | solution.py:172
  76.9 0.8 fusion.46
  78.1 2.8 %shard_map.91 = f32[375,256]{1,0:T(8,128)S(1)} custom-call(s32[16]{0:T(128)S(1)} %fusion.41.pattern_ref, bf16[16,375,375]{2,1,0:T(8,128)(2,1)S(1)} %bitcast.151, bf16[8,375,256]{2,1,0:T(8,128)(2,1)S(1)} %pad_maximum_fusion.values_ref, bf16[375,375]{1,0:T(8,128)(2,1)S(1)} %fusion.19.inverse_ref), custom_call_target="tpu_custom_call" | custom-call | flops 1152000000 | bytes 4500000 | tf_op jit(solution)/shard_map/pallas_call | solution.py:50
  80.9 1.4 %subtract_bitcast_fusion.1 = (f32[1,375,256]{2,1,0:T(8,128)S(1)}, f32[1,375,256]{2,1,0:T(8,128)S(1)}) fusion(f32[375,256]{1,0:T(8,128)S(1)} %fusion.5, f32[375,256]{1,0:T(8,128)S(1)} %shard_map.91, pred[]{:T(512)} %bitcast.28, f32[375,256]{1,0:T(8,128)S(1)} %fusion.4, pred[]{:T(512)} %bitcast.40), kind=kLoop, calls=%fused_computation.41 | loop fusion | flops 384000 | bytes 1920002 | tf_op jit(solution)/shard_map/stack | solution.py:183
  82.3 1.3 %copy.38 = f32[1,2,375,256]{3,1,2,0:T(2,128)} copy(f32[1,2,375,256]{3,2,1,0:T(8,128)S(1)} %maximum_bitcast_fusion) | data formatting | bytes 1536000 | tf_op jit(solution)/shard_map/broadcast_in_dim | solution.py:183
  (73 shorter events, 14.4 us)
Async XLA Ops:
  0.0 8.0 %copy-start = (bf16[1,2,375,375]{3,1,2,0:T(2,128)(2,1)S(1)}, bf16[1,2,375,375]{3,1,2,0:T(2,128)(2,1)}, u32[]{:S(2)}) copy-start(bf16[1,2,375,375]{3,1,2,0:T(2,128)(2,1)} %param.12) | copy-start | bytes 1687504
  0.0 7.9 %copy-start.3 = (bf16[1,2,375,192]{2,3,1,0:T(8,128)(2,1)S(1)}, bf16[1,2,375,192]{2,3,1,0:T(8,128)(2,1)}, u32[]{:S(2)}) copy-start(bf16[1,2,375,192]{2,3,1,0:T(8,128)(2,1)} %param.14) | copy-start | bytes 864004
  0.0 6.5 %copy-start.2 = (f32[1,3,192,192]{3,2,1,0:T(8,128)S(1)}, f32[1,3,192,192]{3,2,1,0:T(8,128)}, u32[]{:S(2)}) copy-start(f32[1,3,192,192]{3,2,1,0:T(8,128)} %param.15) | copy-start | bytes 1327108
  3.5 15.4 %collective-permute-start = (f32[192,256]{1,0:T(8,128)}, f32[192,256]{1,0:T(8,128)}, u32[]{:S(2)}, u32[]{:S(2)}) collective-permute-start(f32[192,256]{1,0:T(8,128)} %convolution_bitcast_fusion.7), channel_id=1, source_target_pairs={{0,1},{2,3},{4,5},{6,7},{8,9},{10,11},{12,13},{14,15},{16,17},{18,... | collective-permute-start | bytes 589832 | tf_op jit(solution)/shard_map/ppermute | solution.py:22
  7.2 14.8 %collective-permute-start.3 = (f32[192,192]{1,0:T(8,128)}, f32[192,192]{1,0:T(8,128)S(1)}, u32[]{:S(2)}, u32[]{:S(2)}) collective-permute-start(f32[192,192]{1,0:T(8,128)} %slice_bitcast_fusion.2), channel_id=1, source_target_pairs={{1,5},{3,7},{5,1},{7,3},{9,13},{11,15},{13,9},{15,11},{17,21},{19,... | collective-permute-start | bytes 442376 | tf_op jit(solution)/shard_map/ppermute | solution.py:22
  8.6 9.2 %copy-start.6 = (s32[1,2,16]{2,1,0:T(2,128)S(1)}, s32[1,2,16]{2,1,0:T(2,128)}, u32[]{:S(2)}) copy-start(s32[1,2,16]{2,1,0:T(2,128)} %param.11) | copy-start | bytes 388
  9.9 10.7 %copy-start.1 = (s32[4]{0:T(128)S(1)}, s32[4]{0:T(128)}, u32[]{:S(2)}) copy-start(s32[4]{0:T(128)} %constant.70.clone) | copy-start | bytes 52
  9.9 44.6 %collective-permute-start.9 = (bf16[375,448]{1,0:T(8,128)(2,1)}, bf16[375,448]{1,0:T(8,128)(2,1)S(1)}, u32[]{:S(2)}, u32[]{:S(2)}) collective-permute-start(bf16[375,448]{1,0:T(8,128)(2,1)} %get-tuple-element.9), channel_id=1, source_target_pairs={{4,8},{5,9},{6,10},{7,11},{8,4},{9,5},{10,6},{11,7},{12,16},{13,17... | collective-permute-start | bytes 1008008 | tf_op jit(solution)/shard_map/ppermute | solution.py:22
  10.8 44.0 %collective-permute-start.10 = (bf16[375,448]{1,0:T(8,128)(2,1)}, bf16[375,448]{1,0:T(8,128)(2,1)}, u32[]{:S(2)}, u32[]{:S(2)}) collective-permute-start(bf16[375,448]{1,0:T(8,128)(2,1)} %get-tuple-element.10), channel_id=1, source_target_pairs={{0,4},{1,5},{2,6},{3,7},{4,0},{5,1},{6,2},{7,3},{8,12},{9,13},{10,... | collective-permute-start | bytes 1008008 | tf_op jit(solution)/shard_map/ppermute | solution.py:22
  19.9 1.4 %collective-permute-start.1 = (bf16[192,256]{1,0:T(8,128)(2,1)S(1)}, bf16[192,256]{1,0:T(8,128)(2,1)S(1)}, u32[]{:S(2)}, u32[]{:S(2)}) collective-permute-start(bf16[192,256]{1,0:T(8,128)(2,1)S(1)} %get-tuple-element.5), channel_id=1, source_target_pairs={{1,3},{3,1},{5,7},{7,5},{9,11},{11,9},{13,15},{15,13},{17,19},{19,... | collective-permute-start | bytes 294920 | tf_op jit(solution)/shard_map/ppermute | solution.py:22
  21.4 1.0 %collective-permute-start.2 = (bf16[192,256]{1,0:T(8,128)(2,1)S(1)}, bf16[192,256]{1,0:T(8,128)(2,1)S(1)}, u32[]{:S(2)}, u32[]{:S(2)}) collective-permute-start(bf16[192,256]{1,0:T(8,128)(2,1)S(1)} %fusion.38), channel_id=1, source_target_pairs={{1,5},{3,7},{5,1},{7,3},{9,13},{11,15},{13,9},{15,11},{17,21},{19,... | collective-permute-start | bytes 294920 | tf_op jit(solution)/shard_map/ppermute | solution.py:22
  24.0 1.4 %collective-permute-start.4 = (bf16[192,256]{1,0:T(8,128)(2,1)S(1)}, bf16[192,256]{1,0:T(8,128)(2,1)S(1)}, u32[]{:S(2)}, u32[]{:S(2)}) collective-permute-start(bf16[192,256]{1,0:T(8,128)(2,1)S(1)} %get-tuple-element.25), channel_id=1, source_target_pairs={{1,9},{3,11},{5,13},{7,15},{9,1},{11,3},{13,5},{15,7},{17,25},{19,... | collective-permute-start | bytes 294920 | tf_op jit(solution)/shard_map/ppermute | solution.py:22
  24.6 5.0 %collective-permute-start.6 = (bf16[192,192]{0,1:T(8,128)(2,1)S(1)}, bf16[192,192]{0,1:T(8,128)(2,1)S(1)}, u32[]{:S(2)}, u32[]{:S(2)}) collective-permute-start(bf16[192,192]{0,1:T(8,128)(2,1)S(1)} %convert_bitcast_fusion.2), channel_id=1, source_target_pairs={{1,9},{3,11},{9,17},{11,19},{13,5},{15,7},{17,25},{19,27},{21,13},... | collective-permute-start | bytes 221192 | tf_op jit(solution)/shard_map/ppermute | solution.py:22
  25.9 3.1 %copy-start.5 = (f32[192,192]{1,0:T(8,128)S(1)}, f32[192,192]{1,0:T(8,128)}, u32[]{:S(2)}) copy-start(f32[192,192]{1,0:T(8,128)} %fusion.44) | copy-start | bytes 442372
  25.9 2.5 %collective-permute-start.5 = (bf16[192,256]{1,0:T(8,128)(2,1)S(1)}, bf16[192,256]{1,0:T(8,128)(2,1)S(1)}, u32[]{:S(2)}, u32[]{:S(2)}) collective-permute-start(bf16[192,256]{1,0:T(8,128)(2,1)S(1)} %get-tuple-element.29), channel_id=1, source_target_pairs={{1,17},{3,19},{5,21},{7,23},{9,25},{11,27},{13,29},{15,31},{17,1},... | collective-permute-start | bytes 294920 | tf_op jit(solution)/shard_map/ppermute | solution.py:22
  27.4 2.2 %collective-permute-start.7 = (bf16[192,256]{1,0:T(8,128)(2,1)S(1)}, bf16[192,256]{1,0:T(8,128)(2,1)S(1)}, u32[]{:S(2)}, u32[]{:S(2)}) collective-permute-start(bf16[192,256]{1,0:T(8,128)(2,1)S(1)} %get-tuple-element.27), channel_id=1, source_target_pairs={{1,9},{3,11},{9,17},{11,19},{13,5},{15,7},{17,25},{19,27},{21,13},... | collective-permute-start | bytes 294920 | tf_op jit(solution)/shard_map/ppermute | solution.py:22
  30.0 24.4 %collective-permute-start.8 = (bf16[3,192,256]{2,1,0:T(8,128)(2,1)S(1)}, bf16[3,192,256]{2,1,0:T(8,128)(2,1)S(1)}, u32[]{:S(2)}, u32[]{:S(2)}) collective-permute-start(bf16[3,192,256]{2,1,0:T(8,128)(2,1)S(1)} %pad_maximum_fusion.5), channel_id=1, source_target_pairs={{1,0},{3,2},{5,4},{7,6},{9,8},{11,10},{13,12},{15,14},{17,16},{19,... | collective-permute-start | bytes 884744 | tf_op jit(solution)/shard_map/ppermute | solution.py:22
  59.8 12.9 %collective-permute-start.11 = (bf16[2,375,256]{2,1,0:T(8,128)(2,1)S(1)}, bf16[2,375,256]{2,1,0:T(8,128)(2,1)S(1)}, u32[]{:S(2)}, u32[]{:S(2)}) collective-permute-start(bf16[2,375,256]{2,1,0:T(8,128)(2,1)S(1)} %pad_maximum_fusion.4), channel_id=1, source_target_pairs={{0,2},{1,3},{2,0},{3,1},{28,30},{29,31},{30,28},{31,29}} | collective-permute-start | bytes 1152008 | tf_op jit(solution)/shard_map/ppermute | solution.py:22
  73.1 4.7 %collective-permute-start.12 = (bf16[4,375,256]{2,0,1:T(4,128)(2,1)S(1)}, bf16[4,375,256]{2,0,1:T(4,128)(2,1)S(1)}, u32[]{:S(2)}, u32[]{:S(2)}) collective-permute-start(bf16[4,375,256]{2,0,1:T(4,128)(2,1)S(1)} %copy.34), channel_id=1, source_target_pairs={{0,1},{1,0},{2,3},{3,2},{28,29},{29,28},{30,31},{31,30}} | collective-permute-start | bytes 2304008 | tf_op jit(solution)/shard_map/ppermute | solution.py:22
  75.8 1.1 %copy-start.4 = (bf16[1,2,375,375]{3,1,2,0:T(2,128)(2,1)S(1)}, bf16[1,2,375,375]{3,1,2,0:T(2,128)(2,1)}, u32[]{:S(2)}) copy-start(bf16[1,2,375,375]{3,1,2,0:T(2,128)(2,1)} %param.13) | copy-start | bytes 1687504

commit v2 on v0

v2 whole, which is shorter than its diff:
```python
import functools

import jax
import jax.numpy as jnp
from jax import lax
from jax.experimental import pallas as pl
from jax.experimental.pallas import tpu as pltpu
from jax.sharding import PartitionSpec as P

HIGHEST = lax.Precision.HIGHEST
BF = jnp.bfloat16
F32 = jnp.float32
VMEM = pl.BlockSpec(memory_space=pltpu.VMEM)
SMEM = pl.BlockSpec(memory_space=pltpu.SMEM)


def route(x, subs, blks, target):
    pairs = []
    for s in range(subs):
        for b in range(blks):
            to = target(s, b)
            if to is not None and 0 <= to[0] < subs:
                pairs.append((s * blks + b, to[0] * blks + to[1]))
    return lax.ppermute(x, ("sub", "blk"), pairs)


def dot(a, b):
    return jnp.dot(a, b, precision=HIGHEST, preferred_element_type=F32)


def tdot(a, b):
    return lax.dot_general(
        a, b, (((0,), (0,)), ((), ())), precision=HIGHEST, preferred_element_type=F32
    )


def bdot(a, b):
    return jnp.dot(a, b, preferred_element_type=F32)


def call(kernel, outs, specs, flops, moved):
    return pl.pallas_call(
        kernel,
        out_shape=outs,
        in_specs=specs,
        out_specs=jax.tree.map(lambda _: VMEM, outs),
        compiler_params=pltpu.CompilerParams(vmem_limit_bytes=32 * 1024 * 1024),
        cost_estimate=pl.CostEstimate(flops=flops, bytes_accessed=moved, transcendentals=0),
    )


def face_kernel(edge_ref, fields_ref, near_ref, far_ref, near_in_ref, far_in_ref, own_ref, near_out, far_out, near_bf, mine_bf):
    loads = own_ref.shape[-1]
    field = fields_ref[0]
    scale = jnp.where(edge_ref[0] > 0, 1.0, 0.5).astype(F32)
    far = (own_ref[1] + bdot(far_ref[:, loads:], field)) * scale
    far_out[...] = far
    mine_bf[0] = far.astype(BF)
    own = own_ref[0] + bdot(near_ref[:, loads:], field)
    other = near_in_ref[:, :loads].astype(F32) + bdot(near_in_ref[:, loads:], fields_ref[1])
    near = 0.5 * own + 0.5 * other
    near_out[...] = near
    near_bf[...] = near.astype(BF)
    mine_bf[1] = near.astype(BF)
    for i in range(far_in_ref.shape[0]):
        block = far_in_ref[i, :, :loads].astype(F32) + bdot(far_in_ref[i, :, loads:], field)
        mine_bf[2 + i] = (block * scale).astype(BF)


def finish_kernel(slots_ref, flags_ref, matrix_ref, inverse_ref, mine_ref, core_ref, late_ref, late_core_ref, far_ref, far_in_ref, near_ref, out_ref, values_ref, total_ref):
    count = mine_ref.shape[0]
    more = late_ref.shape[0]
    is_edge = flags_ref[0] > 0

    @pl.when(is_edge)
    def _():
        values_ref[:count] = mine_ref[...]
        values_ref[count : 2 * count] = core_ref[...]
        values_ref[2 * count : 2 * count + more] = late_ref[...]
        values_ref[2 * count + more :] = late_core_ref[...]
        total = jnp.zeros(total_ref.shape, F32)
        for k in range(matrix_ref.shape[0]):
            total += bdot(matrix_ref[k], values_ref[slots_ref[k]])
        total_ref[...] = far_ref[...] - bdot(inverse_ref[...], total.astype(BF))

    @pl.when(jnp.logical_not(is_edge))
    def _():
        total_ref[...] = far_ref[...] + far_in_ref[...].astype(F32)

    is_even = flags_ref[1] > 0
    far = total_ref[...]
    near = near_ref[...]
    out_ref[0] = jnp.where(is_even, far, near)
    out_ref[1] = jnp.where(is_even, near, far)


def after(x, *others):
    return lax.optimization_barrier((x,) + others)[0]


def shards(subs, blks, residual, stiffness, pattern, neumann_inv, dirichlet_inv, basis, node_ops, root_inv):
    here = lax.axis_index("sub")
    mine = lax.axis_index("blk")
    _, per, block, loads = residual.shape
    width = basis.shape[-1]
    levels = node_ops.shape[1]
    assert per == 2 and levels > 2
    even = here % 2 == 0
    edge = (here == 0) | (here == subs - 1)
    upper = mine % 2 == 1
    go = functools.partial(route, subs=subs, blks=blks)
    others = range(2, blks, 2)

    def swap(x, sub=0, blk=0):
        return go(x, target=lambda s, b: (s ^ sub, b ^ blk))

    local_ids = jnp.arange(per)
    shared = (local_ids == 0) & (here > 0) | (local_ids == per - 1) & (here < subs - 1)
    scale = jnp.where(shared, 0.5, 1.0).astype(F32)[:, None, None]
    scaled_bf = (residual[0] * scale).astype(BF)
    modes = basis[0]
    maps = node_ops[0]

    partial = jnp.einsum("jbm,jbr->mr", modes, scaled_bf, preferred_element_type=F32)
    halves = partial[:, : loads // 2], partial[:, loads // 2 :]
    half = jnp.where(upper, halves[1], halves[0])
    half = half + swap(jnp.where(upper, halves[0], halves[1]), blk=1)
    half_bf = half.astype(BF)

    sibling_map = swap(maps[0], sub=1)

    local_fix = jnp.einsum("jab,jbr->jar", neumann_inv[0], scaled_bf, preferred_element_type=F32)
    local_bf = local_fix.astype(BF)

    coarse = half
    for d in others:
        coarse = coarse + swap(half_bf, blk=d).astype(F32)
    sibling = swap(half_bf, sub=1).astype(F32)
    for d in others:
        sibling = sibling + swap(half_bf, sub=1, blk=d).astype(F32)

    current = tdot(maps[0], coarse) + tdot(sibling_map, sibling)
    own = tdot(maps[1], current)
    own_bf = own.astype(BF)
    quad = own + swap(own_bf, sub=2).astype(F32)
    other_map = swap(maps[2], sub=4)
    other_quad = swap(own_bf, sub=4).astype(F32) + swap(own_bf, sub=6).astype(F32)
    payload = [jnp.concatenate([local_bf[j], modes[j]], axis=1) for j in range(per)]
    to_sibling = jnp.where(even, payload[1], payload[0])
    to_far = jnp.where(even, payload[0], payload[1])
    to_sibling, to_far = after(to_sibling, coarse, sibling), after(to_far, coarse, sibling)
    from_sibling = swap(to_sibling, sub=1)
    from_others = jnp.stack([swap(to_far, blk=d) for d in others])
    values = [coarse, current, quad]
    current = tdot(maps[2], quad) + tdot(other_map, other_quad)
    for level in range(3, levels):
        values.append(current)
        own = tdot(maps[level], current)
        current = own + swap(own.astype(BF), sub=2**level).astype(F32)
    field = dot(root_inv, current)
    for level in reversed(range(1, levels)):
        field = dot(maps[level], field) + values[level]
    fields = jnp.stack([dot(maps[0], field) + coarse, dot(sibling_map, field) + sibling]).astype(BF)
    across = swap(fields, blk=1)
    fields = jnp.concatenate(
        [jnp.where(upper, across, fields), jnp.where(upper, fields, across)], axis=2
    )

    shape = jax.ShapeDtypeStruct
    count = 2 + len(others)
    near, far, near_bf, mine_bf = call(
        face_kernel,
        (
            shape((block, loads), F32),
            shape((block, loads), F32),
            shape((block, loads), BF),
            shape((count, block, loads), BF),
        ),
        [SMEM] + [VMEM] * 6,
        2 * (count + 1) * block * width * loads,
        count * block * loads * 8,
    )(
        edge.astype(jnp.int32)[None],
        fields,
        to_sibling,
        to_far,
        from_sibling,
        from_others,
        jnp.where(even, local_fix[::-1], local_fix),
    )

    late = jnp.stack([swap(near_bf, blk=d) for d in others])
    core = swap(mine_bf, blk=1)
    far_in = go(
        mine_bf[0],
        target=lambda s, b: (s - 1 if s % 2 == 0 else s + 1, b),
    )
    late_core = swap(late, blk=1)
    slot = {(0, 0): 0, (0, 1): 1, (1, 0): count, (1, 1): count + 1}
    for i, d in enumerate(others):
        slot[d, 0], slot[d ^ 1, 0] = 2 + i, count + 2 + i
        slot[d, 1], slot[d ^ 1, 1] = 2 * count + i, 2 * count + len(others) + i
    table = jnp.array([[slot[d, k] for k in range(2)] for d in range(blks)], jnp.int32)
    far_id = jnp.where(even, 0, per - 1)
    columns = pattern[0, far_id]
    slots = table[(columns // per) ^ mine, (columns % per != far_id).astype(jnp.int32)]
    result = pl.pallas_call(
        finish_kernel,
        out_shape=shape((per, block, loads), F32),
        in_specs=[SMEM, SMEM] + [VMEM] * 9,
        out_specs=VMEM,
        scratch_shapes=[
            pltpu.VMEM((blks * per, block, loads), BF),
            pltpu.VMEM((block, loads), F32),
        ],
        compiler_params=pltpu.CompilerParams(vmem_limit_bytes=32 * 1024 * 1024),
        cost_estimate=pl.CostEstimate(
            flops=2 * pattern.shape[-1] * block * block * loads,
            bytes_accessed=2 * pattern.shape[-1] * block * block,
            transcendentals=0,
        ),
    )(
        slots,
        jnp.stack([edge, even]).astype(jnp.int32),
        lax.dynamic_index_in_dim(stiffness[0], far_id, 0, False),
        lax.dynamic_index_in_dim(dirichlet_inv[0], far_id, 0, False),
        mine_bf,
        core,
        late,
        late_core,
        far,
        far_in,
        near,
    )
    return result[None]


def solution(mesh):
    placed = (
        P("sub", "blk", None, None),
        P("sub", "blk", None, None, None),
        P("sub", "blk", None),
        P("sub", "blk", None, None),
        P("sub", "blk", None, None),
        P("sub", "blk", None, None),
        P("sub", None, None, None),
        P(),
    )
    return jax.shard_map(
        functools.partial(shards, mesh.shape["sub"], mesh.shape["blk"]),
        mesh=mesh,
        in_specs=placed,
        out_specs=P("sub", "blk", None, None),
        check_vma=False,
    )
```

time: 136 us -> 71.4 us (0.53)
  waiting for transfers between devices: 72.7 us -> 18.7 us
  matrix products: 22.8 us -> 6.86 us
  between operations: 13.6 us -> 0.28 us
  local copies, waits for them, and re-layouts: 7.19 us -> 20.2 us
  starting transfers between devices: 10.3 us -> 18.7 us
  blocking collectives: 5.42 us -> 0 us
  Pallas kernels: 0 us -> 3.35 us
    unnamed x3 -> x0, waiting for transfers between devices: 23.5 us -> none
    all_gather x1 -> x0, waiting for transfers between devices: 20.5 us -> none  [shards(): gathered = lax.all_gather(assembled_bf, 'blk', axis=1, tiled=True)]
    dot_general x10 -> x11, matrix products: 22.4 us -> 6.49 us  [the longest x5 3.62 us: tdot(): lax.dot_general(a, b, (((0,), (0,)), ((), ())), precision=HIGHEST, prefer...]
    dynamic_slice x0 -> x3, local copies, waits for them, and re-layouts: none -> 11 us  [the longest x2 10.4 us: shards(): lax.dynamic_index_in_dim(stiffness[0], far_id, 0, False)]
    ppermute x5 -> x16, waiting for transfers between devices: 28.7 us -> 18.7 us  [route(): return lax.ppermute(x, ('sub', 'blk'), pairs)]
    ppermute x5 -> x16, starting transfers between devices: 10.3 us -> 18.7 us  [route(): return lax.ppermute(x, ('sub', 'blk'), pairs)]
    all_gather x1 -> x0, blocking collectives: 5.42 us -> none  [shards(): lax.all_gather(field.astype(jnp.bfloat16), 'blk', axis=1, tiled=True)]
    gather x1, local copies, waits for them, and re-layouts: 5.02 us -> 0.68 us  [shards(): table[columns // per ^ mine, (columns % per != far_id).astype(jnp.int32)]]
  transfers between devices with their start and end apart: 7 -> 16, of which waited for: 7 -> 6; matrix products, arithmetic and copies ran while one was open for 0% -> 32% of each run, Pallas kernels for 0% -> 0%
where the time goes in v2:
time: 71.4 us; the launch traced here: 71.1 us
  local copies, waits for them, and re-layouts  20.2 us (28%)
  starting transfers between devices  18.7 us (26%)
  waiting for transfers between devices  18.7 us (26%)
  matrix products  6.86 us (10%)
  Pallas kernels  3.35 us (5%)
  other arithmetic  3.02 us (4%)
    ppermute x16, starting transfers between devices, route(): return lax.ppermute(x, ('sub', 'blk'), pairs)  18.7 us
    ppermute x16, waiting for transfers between devices, route(): return lax.ppermute(x, ('sub', 'blk'), pairs)  18.7 us
    dynamic_slice x2, local copies, waits for them, and re-layouts, shards(): lax.dynamic_index_in_dim(stiffness[0], far_id, 0, False)  10.4 us
    unnamed x19, local copies, waits for them, and re-layouts  4.02 us
    dot_general x5, matrix products, tdot(): lax.dot_general(a, b, (((0,), (0,)), ((), ())), precision=HIGHEST, prefer...  3.62 us
    pallas_call x1, Pallas kernels, shards(): pl.pallas_call(finish_kernel, out_shape=shape((per, block, loads), F32),...  2.96 us
    squeeze x1, local copies, waits for them, and re-layouts, shards(): field = dot(maps[level], field) + values[level]  1.8 us
    dot_general x5, matrix products, dot(): return jnp.dot(a, b, precision=HIGHEST, preferred_element_type=F32)  1.64 us
  transfers between devices with their start and end apart: 16, of which 6 were waited for; matrix products, arithmetic and copies ran while one was open for 32% of the time, Pallas kernels for 0%

profile of v2, /device:TPU:0, one launch (start us, length us, event | category | flops | bytes accessed | tf_op | source)
XLA Modules:
  0.0 71.1 jit_solution(14054221325193128739)
XLA Ops:
  0.0 1.8 %slice_bitcast_fusion = (f32[192,192]{1,0:T(8,128)}, f32[192,192]{1,0:T(8,128)S(1)}) fusion(f32[1,3,192,192]{3,2,1,0:T(8,128)} %param.15), kind=kLoop, calls=%fused_computation.33 | loop fusion | bytes 589824 | tf_op jit(solution)/shard_map/squeeze | solution.py:162
  1.8 2.9 %collective-permute-start.4 = (f32[192,192]{1,0:T(8,128)S(1)}, f32[192,192]{1,0:T(8,128)S(1)}, u32[]{:S(2)}, u32[]{:S(2)}) collective-permute-start(f32[192,192]{1,0:T(8,128)S(1)} %get-tuple-element.24), channel_id=1, source_target_pairs={{0,4},{1,5},{2,6},{3,7},{4,0},{5,1},{6,2},{7,3},{8,12},{9,13},{10,... | collective-permute-start | bytes 442376 | tf_op jit(solution)/shard_map/ppermute | solution.py:24
  4.8 1.5 %fusion.7 = bf16[2,375,256]{2,0,1:T(2,128)(2,1)S(1)} fusion(f32[1,2,375,256]{3,1,2,0:T(2,128)} %param.9, f32[2]{0:T(128)S(1)} %or_select_fusion), kind=kLoop, calls=%fused_computation.20 | loop fusion | flops 384000 | bytes 1152008 | tf_op jit(solution)/shard_map/convert_element_type | solution.py:120
  6.2 1.2 %convolution_bitcast_fusion.1 = f32[192,256]{1,0:T(8,128)S(1)} fusion(bf16[2,375,256]{2,0,1:T(2,128)(2,1)S(1)} %fusion.7, bf16[1,2,375,192]{2,3,1,0:T(8,128)(2,1)} %param.14), kind=kOutput, calls=%fused_computation.4 | convolution fusion | flops 73728000 | bytes 868608 | tf_op jit(solution)/shard_map/jbm,jbr->mr/dot_general | solution.py:124
  7.6 2.6 %collective-permute-start.8 = (f32[192,192]{1,0:T(8,128)}, f32[192,192]{1,0:T(8,128)}, u32[]{:S(2)}, u32[]{:S(2)}) collective-permute-start(f32[192,192]{1,0:T(8,128)} %get-tuple-element.23), channel_id=1, source_target_pairs={{0,16},{1,17},{2,18},{3,19},{4,20},{5,21},{6,22},{7,23},{8,24},{9,... | collective-permute-start | bytes 442376 | tf_op jit(solution)/shard_map/ppermute | solution.py:24
  11.5 1.6 %collective-permute-start.1 = (bf16[192,128]{1,0:T(8,128)(2,1)S(1)}, bf16[192,128]{1,0:T(8,128)(2,1)S(1)}, u32[]{:S(2)}, u32[]{:S(2)}) collective-permute-start(bf16[192,128]{1,0:T(8,128)(2,1)S(1)} %get-tuple-element.17), channel_id=1, source_target_pairs={{0,2},{1,3},{2,0},{3,1},{4,6},{5,7},{6,4},{7,5},{8,10},{9,11},{10,... | collective-permute-start | bytes 147464 | tf_op jit(solution)/shard_map/ppermute | solution.py:24
  13.1 4.9 %constant_dynamic-slice_fusion.1 = bf16[1,1,16,375,375]{4,2,3,1,0:T(8,128)(2,1)} fusion(bf16[1,2,16,375,375]{4,2,3,1,0:T(8,128)(2,1)} %param.10, s32[]{:T(128)S(6)} %select_n.118), kind=kLoop, calls=%fused_computation.63 | loop fusion | bytes 9000004 | tf_op jit(solution)/shard_map/jit(dynamic_index_in_dim)/dynamic_slice | solution.py:225
  20.1 1.5 %collective-permute-start.2 = (bf16[192,128]{1,0:T(8,128)(2,1)S(1)}, bf16[192,128]{1,0:T(8,128)(2,1)S(1)}, u32[]{:S(2)}, u32[]{:S(2)}) collective-permute-start(bf16[192,128]{1,0:T(8,128)(2,1)S(1)} %get-tuple-element.17), channel_id=1, source_target_pairs={{0,4},{1,5},{2,6},{3,7},{4,0},{5,1},{6,2},{7,3},{8,12},{9,13},{10,... | collective-permute-start | bytes 147464 | tf_op jit(solution)/shard_map/ppermute | solution.py:24
  21.6 3.0 %collective-permute-done.3 = bf16[192,128]{1,0:T(8,128)(2,1)S(1)} collective-permute-done((bf16[192,128]{1,0:T(8,128)(2,1)S(1)}, bf16[192,128]{1,0:T(8,128)(2,1)S(1)}, u32[]{:S(2)}, u32[]{:S(2)}) %collective-permute-start.3) | collective-permute-done | bytes 49184 | tf_op jit(solution)/shard_map/ppermute | solution.py:24
  26.4 1.4 %collective-permute-start.7 = (bf16[192,128]{1,0:T(8,128)(2,1)S(1)}, bf16[192,128]{1,0:T(8,128)(2,1)}, u32[]{:S(2)}, u32[]{:S(2)}) collective-permute-start(bf16[192,128]{1,0:T(8,128)(2,1)S(1)} %get-tuple-element.31), channel_id=1, source_target_pairs={{0,24},{1,25},{2,26},{3,27},{4,28},{5,29},{6,30},{7,31},{8,16},{9,... | collective-permute-start | bytes 147464 | tf_op jit(solution)/shard_map/ppermute | solution.py:24
  27.8 1.7 %collective-permute-start.6 = (bf16[192,128]{1,0:T(8,128)(2,1)S(1)}, bf16[192,128]{1,0:T(8,128)(2,1)}, u32[]{:S(2)}, u32[]{:S(2)}) collective-permute-start(bf16[192,128]{1,0:T(8,128)(2,1)S(1)} %get-tuple-element.31), channel_id=1, source_target_pairs={{0,16},{1,17},{2,18},{3,19},{4,20},{5,21},{6,22},{7,23},{8,24},{9,... | collective-permute-start | bytes 147464 | tf_op jit(solution)/shard_map/ppermute | solution.py:24
  29.5 1.3 %broadcast_select_fusion = (bf16[375,448]{1,0:T(8,128)(2,1)S(1)}, bf16[375,448]{1,0:T(8,128)(2,1)S(1)}) fusion(pred[]{:T(512)} %eq.31, bf16[375,192]{1,0:T(8,128)(2,1)} %bitcast.98, bf16[375,256]{1,0:T(8,128)(2,1)} %get-tuple-element.26, bf16[375,192]{1,0:T(8,128)(2,1)} %bitcast.99, bf16[375,256]{1,0:T(8,128)(2,1)S(1)} %get-tuple-element.25), kind=kLoop, calls=%fused_computation.24 | loop fusion | flops 1680000 | bytes 1344001 | tf_op jit(solution)/shard_map/jit(_where)/select_n | solution.py:150
  30.8 5.5 %copy.36 = bf16[1,1,16,375,375]{4,3,2,1,0:T(8,128)(2,1)} copy(bf16[1,1,16,375,375]{4,2,3,1,0:T(8,128)(2,1)} %constant_dynamic-slice_fusion.1) | data formatting | bytes 9000000 | tf_op jit(solution)/shard_map/jit(dynamic_index_in_dim)/dynamic_slice | solution.py:225
  36.2 1.4 %collective-permute-start.5 = (bf16[192,128]{1,0:T(8,128)(2,1)S(1)}, bf16[192,128]{1,0:T(8,128)(2,1)S(1)}, u32[]{:S(2)}, u32[]{:S(2)}) collective-permute-start(bf16[192,128]{1,0:T(8,128)(2,1)S(1)} %get-tuple-element.31), channel_id=1, source_target_pairs={{0,8},{1,9},{2,10},{3,11},{4,12},{5,13},{6,14},{7,15},{8,0},{9,1},... | collective-permute-start | bytes 147464 | tf_op jit(solution)/shard_map/ppermute | solution.py:24
  37.6 1.4 %fusion.16 = f32[128,192]{1,0:T(8,128)S(1)} fusion(f32[192,192]{1,0:T(8,128)} %collective-permute-done.8, bf16[192,128]{1,0:T(8,128)(2,1)} %collective-permute-done.7, bf16[192,128]{1,0:T(8,128)(2,1)} %collective-permute-done.6), kind=kOutput, calls=%fused_computation.41 | convolution fusion | flops 56696832 | bytes 344064 | tf_op jit(solution)/shard_map/dot_general | solution.py:32
  39.1 1.3 %collective-permute-done.5 = bf16[192,128]{1,0:T(8,128)(2,1)S(1)} collective-permute-done((bf16[192,128]{1,0:T(8,128)(2,1)S(1)}, bf16[192,128]{1,0:T(8,128)(2,1)S(1)}, u32[]{:S(2)}, u32[]{:S(2)}) %collective-permute-start.5) | collective-permute-done | bytes 49184 | tf_op jit(solution)/shard_map/ppermute | solution.py:24
  42.6 1.1 %collective-permute-start.10 = (bf16[375,448]{1,0:T(8,128)(2,1)S(1)}, bf16[375,448]{1,0:T(8,128)(2,1)S(1)}, u32[]{:S(2)}, u32[]{:S(2)}) collective-permute-start(bf16[375,448]{1,0:T(8,128)(2,1)S(1)} %get-tuple-element.11.near_ref), channel_id=1, source_target_pairs={{0,4},{1,5},{2,6},{3,7},{4,0},{5,1},{6,2},{7,3},{8,12},{9,13},{10,... | collective-permute-start | bytes 1008008 | tf_op jit(solution)/shard_map/ppermute | solution.py:24
  43.7 1.5 %collective-permute-start.11 = (bf16[375,448]{1,0:T(8,128)(2,1)S(1)}, bf16[375,448]{1,0:T(8,128)(2,1)S(1)}, u32[]{:S(2)}, u32[]{:S(2)}) collective-permute-start(bf16[375,448]{1,0:T(8,128)(2,1)S(1)} %get-tuple-element.12.far_ref), channel_id=1, source_target_pairs={{0,2},{1,3},{2,0},{3,1},{4,6},{5,7},{6,4},{7,5},{8,10},{9,11},{10,... | collective-permute-start | bytes 1008008 | tf_op jit(solution)/shard_map/ppermute | solution.py:24
  45.3 8.6 %collective-permute-done.10.near_in_ref = bf16[375,448]{1,0:T(8,128)(2,1)S(1)} collective-permute-done((bf16[375,448]{1,0:T(8,128)(2,1)S(1)}, bf16[375,448]{1,0:T(8,128)(2,1)S(1)}, u32[]{:S(2)}, u32[]{:S(2)}) %collective-permute-start.10) | collective-permute-done | bytes 336032 | tf_op jit(solution)/shard_map/ppermute | solution.py:24
  55.9 1.6 %collective-permute-start.13 = (bf16[375,256]{1,0:T(8,128)(2,1)S(1)}, bf16[375,256]{1,0:T(8,128)(2,1)S(1)}, u32[]{:S(2)}, u32[]{:S(2)}) collective-permute-start(bf16[375,256]{1,0:T(8,128)(2,1)S(1)} %get-tuple-element.14), channel_id=1, source_target_pairs={{0,2},{1,3},{2,0},{3,1},{4,6},{5,7},{6,4},{7,5},{8,10},{9,11},{10,... | collective-permute-start | bytes 576008 | tf_op jit(solution)/shard_map/ppermute | solution.py:24
  58.8 4.3 %collective-permute-done.13 = bf16[375,256]{1,0:T(8,128)(2,1)S(1)} collective-permute-done((bf16[375,256]{1,0:T(8,128)(2,1)S(1)}, bf16[375,256]{1,0:T(8,128)(2,1)S(1)}, u32[]{:S(2)}, u32[]{:S(2)}) %collective-permute-start.13) | collective-permute-done | bytes 192032 | tf_op jit(solution)/shard_map/ppermute | solution.py:24
  64.6 2.3 %copy-done.1 = bf16[1,1,16,375,375]{4,3,2,1,0:T(8,128)(2,1)S(1)} copy-done((bf16[1,1,16,375,375]{4,3,2,1,0:T(8,128)(2,1)S(1)}, bf16[1,1,16,375,375]{4,3,2,1,0:T(8,128)(2,1)}, u32[]{:S(2)}) %copy-start.1) | copy-done | bytes 4500024
  66.9 3.0 %shard_map.92 = f32[2,375,256]{2,1,0:T(8,128)S(1)} custom-call(s32[16]{0:T(128)S(1)} %gather_fusion, s32[2]{0:T(128)S(1)} %add_convert_fusion.flags_ref, bf16[16,375,375]{2,1,0:T(8,128)(2,1)S(1)} %bitcast.92, bf16[375,375]{1,0:T(8,128)(2,1)S(1)} %bitcast.94, bf16[3,375,256]{2,1,0:T(8,128)(2,1)S(1)} %get-tuple-element.13.mine_ref, ...), custom_call_target="tpu_custom_call" | custom-call | flops 1152000000 | bytes 4500000 | tf_op jit(solution)/shard_map/pallas_call | solution.py:207
  69.8 1.3 %copy.24 = f32[1,2,375,256]{3,1,2,0:T(2,128)} copy(f32[1,2,375,256]{3,2,1,0:T(8,128)S(1)} %bitcast.93) | data formatting | bytes 1536000 | tf_op jit(solution)/shard_map/broadcast_in_dim | solution.py:235
  (62 shorter events, 12.1 us)
Async XLA Ops:
  0.0 10.2 %copy-start = (bf16[1,2,375,375]{3,1,2,0:T(2,128)(2,1)S(1)}, bf16[1,2,375,375]{3,1,2,0:T(2,128)(2,1)}, u32[]{:S(2)}) copy-start(bf16[1,2,375,375]{3,1,2,0:T(2,128)(2,1)} %param.12) | copy-start | bytes 1687504
  0.0 11.4 %copy-start.4 = (bf16[1,2,375,192]{2,3,1,0:T(8,128)(2,1)S(1)}, bf16[1,2,375,192]{2,3,1,0:T(8,128)(2,1)}, u32[]{:S(2)}) copy-start(bf16[1,2,375,192]{2,3,1,0:T(8,128)(2,1)} %param.14) | copy-start | bytes 864004
  1.8 19.8 %collective-permute-start.4 = (f32[192,192]{1,0:T(8,128)S(1)}, f32[192,192]{1,0:T(8,128)S(1)}, u32[]{:S(2)}, u32[]{:S(2)}) collective-permute-start(f32[192,192]{1,0:T(8,128)S(1)} %get-tuple-element.24), channel_id=1, source_target_pairs={{0,4},{1,5},{2,6},{3,7},{4,0},{5,1},{6,2},{7,3},{8,12},{9,13},{10,... | collective-permute-start | bytes 442376 | tf_op jit(solution)/shard_map/ppermute | solution.py:24
  7.5 3.9 %collective-permute-start = (f32[192,128]{1,0:T(8,128)S(1)}, f32[192,128]{1,0:T(8,128)S(1)}, u32[]{:S(2)}, u32[]{:S(2)}) collective-permute-start(f32[192,128]{1,0:T(8,128)S(1)} %slice_select_fusion), channel_id=1, source_target_pairs={{0,1},{1,0},{2,3},{3,2},{4,5},{5,4},{6,7},{7,6},{8,9},{9,8},{10,11... | collective-permute-start | bytes 294920 | tf_op jit(solution)/shard_map/ppermute | solution.py:24
  7.6 30.1 %collective-permute-start.8 = (f32[192,192]{1,0:T(8,128)}, f32[192,192]{1,0:T(8,128)}, u32[]{:S(2)}, u32[]{:S(2)}) collective-permute-start(f32[192,192]{1,0:T(8,128)} %get-tuple-element.23), channel_id=1, source_target_pairs={{0,16},{1,17},{2,18},{3,19},{4,20},{5,21},{6,22},{7,23},{8,24},{9,... | collective-permute-start | bytes 442376 | tf_op jit(solution)/shard_map/ppermute | solution.py:24
  11.5 13.8 %copy-start.3 = (f32[1,3,192,192]{3,2,1,0:T(8,128)S(1)}, f32[1,3,192,192]{3,2,1,0:T(8,128)}, u32[]{:S(2)}) copy-start(f32[1,3,192,192]{3,2,1,0:T(8,128)} %param.15) | copy-start | bytes 1327108
  11.5 10.1 %collective-permute-start.1 = (bf16[192,128]{1,0:T(8,128)(2,1)S(1)}, bf16[192,128]{1,0:T(8,128)(2,1)S(1)}, u32[]{:S(2)}, u32[]{:S(2)}) collective-permute-start(bf16[192,128]{1,0:T(8,128)(2,1)S(1)} %get-tuple-element.17), channel_id=1, source_target_pairs={{0,2},{1,3},{2,0},{3,1},{4,6},{5,7},{6,4},{7,5},{8,10},{9,11},{10,... | collective-permute-start | bytes 147464 | tf_op jit(solution)/shard_map/ppermute | solution.py:24
  19.6 5.0 %collective-permute-start.3 = (bf16[192,128]{1,0:T(8,128)(2,1)S(1)}, bf16[192,128]{1,0:T(8,128)(2,1)S(1)}, u32[]{:S(2)}, u32[]{:S(2)}) collective-permute-start(bf16[192,128]{1,0:T(8,128)(2,1)S(1)} %get-tuple-element.17), channel_id=1, source_target_pairs={{0,6},{1,7},{2,4},{3,5},{4,2},{5,3},{6,0},{7,1},{8,14},{9,15},{10,... | collective-permute-start | bytes 147464 | tf_op jit(solution)/shard_map/ppermute | solution.py:24
  20.1 4.5 %collective-permute-start.2 = (bf16[192,128]{1,0:T(8,128)(2,1)S(1)}, bf16[192,128]{1,0:T(8,128)(2,1)S(1)}, u32[]{:S(2)}, u32[]{:S(2)}) collective-permute-start(bf16[192,128]{1,0:T(8,128)(2,1)S(1)} %get-tuple-element.17), channel_id=1, source_target_pairs={{0,4},{1,5},{2,6},{3,7},{4,0},{5,1},{6,2},{7,3},{8,12},{9,13},{10,... | collective-permute-start | bytes 147464 | tf_op jit(solution)/shard_map/ppermute | solution.py:24
  26.4 11.2 %collective-permute-start.7 = (bf16[192,128]{1,0:T(8,128)(2,1)S(1)}, bf16[192,128]{1,0:T(8,128)(2,1)}, u32[]{:S(2)}, u32[]{:S(2)}) collective-permute-start(bf16[192,128]{1,0:T(8,128)(2,1)S(1)} %get-tuple-element.31), channel_id=1, source_target_pairs={{0,24},{1,25},{2,26},{3,27},{4,28},{5,29},{6,30},{7,31},{8,16},{9,... | collective-permute-start | bytes 147464 | tf_op jit(solution)/shard_map/ppermute | solution.py:24
  27.8 9.8 %collective-permute-start.6 = (bf16[192,128]{1,0:T(8,128)(2,1)S(1)}, bf16[192,128]{1,0:T(8,128)(2,1)}, u32[]{:S(2)}, u32[]{:S(2)}) collective-permute-start(bf16[192,128]{1,0:T(8,128)(2,1)S(1)} %get-tuple-element.31), channel_id=1, source_target_pairs={{0,16},{1,17},{2,18},{3,19},{4,20},{5,21},{6,22},{7,23},{8,24},{9,... | collective-permute-start | bytes 147464 | tf_op jit(solution)/shard_map/ppermute | solution.py:24
  30.8 10.0 %copy-start.6 = (f32[192,192]{1,0:T(8,128)S(1)}, f32[192,192]{1,0:T(8,128)}, u32[]{:S(2)}) copy-start(f32[192,192]{1,0:T(8,128)} %param.16) | copy-start | bytes 442372
  36.2 19.0 %copy-start.5 = (bf16[1,2,375,375]{3,1,2,0:T(2,128)(2,1)S(1)}, bf16[1,2,375,375]{3,1,2,0:T(2,128)(2,1)}, u32[]{:S(2)}) copy-start(bf16[1,2,375,375]{3,1,2,0:T(2,128)(2,1)} %param.13) | copy-start | bytes 1687504
  36.2 26.9 %copy-start.7 = (s32[1,2,16]{2,1,0:T(2,128)S(1)}, s32[1,2,16]{2,1,0:T(2,128)}, u32[]{:S(2)}) copy-start(s32[1,2,16]{2,1,0:T(2,128)} %param.11) | copy-start | bytes 388
  36.2 26.9 %copy-start.2 = (s32[4,2]{1,0:T(4,128)S(1)}, s32[4,2]{1,0:T(4,128)}, u32[]{:S(2)}) copy-start(s32[4,2]{1,0:T(4,128)} %constant.72.clone) | copy-start | bytes 100
  36.2 4.1 %collective-permute-start.5 = (bf16[192,128]{1,0:T(8,128)(2,1)S(1)}, bf16[192,128]{1,0:T(8,128)(2,1)S(1)}, u32[]{:S(2)}, u32[]{:S(2)}) collective-permute-start(bf16[192,128]{1,0:T(8,128)(2,1)S(1)} %get-tuple-element.31), channel_id=1, source_target_pairs={{0,8},{1,9},{2,10},{3,11},{4,12},{5,13},{6,14},{7,15},{8,0},{9,1},... | collective-permute-start | bytes 147464 | tf_op jit(solution)/shard_map/ppermute | solution.py:24
  42.5 2.7 %collective-permute-start.9 = (bf16[2,192,128]{2,1,0:T(8,128)(2,1)S(1)}, bf16[2,192,128]{2,1,0:T(8,128)(2,1)S(1)}, u32[]{:S(2)}, u32[]{:S(2)}) collective-permute-start(bf16[2,192,128]{2,1,0:T(8,128)(2,1)S(1)} %pad_maximum_fusion.3), channel_id=1, source_target_pairs={{0,1},{1,0},{2,3},{3,2},{4,5},{5,4},{6,7},{7,6},{8,9},{9,8},{10,11... | collective-permute-start | bytes 294920 | tf_op jit(solution)/shard_map/ppermute | solution.py:24
  42.6 11.4 %collective-permute-start.10 = (bf16[375,448]{1,0:T(8,128)(2,1)S(1)}, bf16[375,448]{1,0:T(8,128)(2,1)S(1)}, u32[]{:S(2)}, u32[]{:S(2)}) collective-permute-start(bf16[375,448]{1,0:T(8,128)(2,1)S(1)} %get-tuple-element.11.near_ref), channel_id=1, source_target_pairs={{0,4},{1,5},{2,6},{3,7},{4,0},{5,1},{6,2},{7,3},{8,12},{9,13},{10,... | collective-permute-start | bytes 1008008 | tf_op jit(solution)/shard_map/ppermute | solution.py:24
  43.7 11.0 %collective-permute-start.11 = (bf16[375,448]{1,0:T(8,128)(2,1)S(1)}, bf16[375,448]{1,0:T(8,128)(2,1)S(1)}, u32[]{:S(2)}, u32[]{:S(2)}) collective-permute-start(bf16[375,448]{1,0:T(8,128)(2,1)S(1)} %get-tuple-element.12.far_ref), channel_id=1, source_target_pairs={{0,2},{1,3},{2,0},{3,1},{4,6},{5,7},{6,4},{7,5},{8,10},{9,11},{10,... | collective-permute-start | bytes 1008008 | tf_op jit(solution)/shard_map/ppermute | solution.py:24
  55.1 9.5 %collective-permute-start.12 = (bf16[3,375,256]{2,1,0:T(8,128)(2,1)S(1)}, bf16[3,375,256]{2,1,0:T(8,128)(2,1)S(1)}, u32[]{:S(2)}, u32[]{:S(2)}) collective-permute-start(bf16[3,375,256]{2,1,0:T(8,128)(2,1)S(1)} %get-tuple-element.13.mine_ref), channel_id=1, source_target_pairs={{0,1},{1,0},{2,3},{3,2},{4,5},{5,4},{6,7},{7,6},{8,9},{9,8},{10,11... | collective-permute-start | bytes 1728008 | tf_op jit(solution)/shard_map/ppermute | solution.py:24
  55.9 7.3 %collective-permute-start.13 = (bf16[375,256]{1,0:T(8,128)(2,1)S(1)}, bf16[375,256]{1,0:T(8,128)(2,1)S(1)}, u32[]{:S(2)}, u32[]{:S(2)}) collective-permute-start(bf16[375,256]{1,0:T(8,128)(2,1)S(1)} %get-tuple-element.14), channel_id=1, source_target_pairs={{0,2},{1,3},{2,0},{3,1},{4,6},{5,7},{6,4},{7,5},{8,10},{9,11},{10,... | collective-permute-start | bytes 576008 | tf_op jit(solution)/shard_map/ppermute | solution.py:24
  58.1 5.8 %collective-permute-start.15 = (bf16[375,256]{1,0:T(8,128)(2,1)}, bf16[375,256]{1,0:T(8,128)(2,1)S(1)}, u32[]{:S(2)}, u32[]{:S(2)}) collective-permute-start(bf16[375,256]{1,0:T(8,128)(2,1)} %slice_bitcast_fusion.4), channel_id=1, source_target_pairs={{4,8},{5,9},{6,10},{7,11},{8,4},{9,5},{10,6},{11,7},{12,16},{13,17... | collective-permute-start | bytes 576008 | tf_op jit(solution)/shard_map/ppermute | solution.py:24
  63.1 1.4 %collective-permute-start.14 = (bf16[1,375,256]{2,1,0:T(8,128)(2,1)S(1)}, bf16[1,375,256]{2,1,0:T(8,128)(2,1)S(1)}, u32[]{:S(2)}, u32[]{:S(2)}) collective-permute-start(bf16[1,375,256]{2,1,0:T(8,128)(2,1)S(1)} %bitcast.96), channel_id=1, source_target_pairs={{0,1},{1,0},{2,3},{3,2},{4,5},{5,4},{6,7},{7,6},{8,9},{9,8},{10,11... | collective-permute-start | bytes 576008 | tf_op jit(solution)/shard_map/ppermute | solution.py:24
  64.6 2.3 %copy-start.1 = (bf16[1,1,16,375,375]{4,3,2,1,0:T(8,128)(2,1)S(1)}, bf16[1,1,16,375,375]{4,3,2,1,0:T(8,128)(2,1)}, u32[]{:S(2)}) copy-start(bf16[1,1,16,375,375]{4,3,2,1,0:T(8,128)(2,1)} %copy.36) | copy-start | bytes 13500004

commit v3 on v2

v3 whole, which is shorter than its diff:
```python
import functools

import jax
import jax.numpy as jnp
from jax import lax
from jax.experimental import pallas as pl
from jax.experimental.pallas import tpu as pltpu
from jax.sharding import PartitionSpec as P

BF = jnp.bfloat16
F32 = jnp.float32
VMEM = pl.BlockSpec(memory_space=pltpu.VMEM)
SMEM = pl.BlockSpec(memory_space=pltpu.SMEM)
HBM = pl.BlockSpec(memory_space=pltpu.HBM)


def route(x, subs, blks, target):
    pairs = []
    for s in range(subs):
        for b in range(blks):
            to = target(s, b)
            if to is not None and 0 <= to[0] < subs:
                pairs.append((s * blks + b, to[0] * blks + to[1]))
    return lax.ppermute(x, ("sub", "blk"), pairs)


def product(a, b, dims):
    a_high, b_high = a.astype(BF), b.astype(BF)
    a_low, b_low = (a - a_high.astype(F32)).astype(BF), (b - b_high.astype(F32)).astype(BF)
    part = functools.partial(
        lax.dot_general, dimension_numbers=(dims, ((), ())), preferred_element_type=F32
    )
    return part(a_high, b_high) + (part(a_high, b_low) + part(a_low, b_high))


def dot(a, b):
    return product(a, b, ((1,), (0,)))


def tdot(a, b):
    return product(a, b, ((0,), (0,)))


def bdot(a, b):
    return jnp.dot(a, b, preferred_element_type=F32)


def call(kernel, outs, specs, flops, moved, scratch=(), limit=16):
    return pl.pallas_call(
        kernel,
        out_shape=outs,
        in_specs=specs,
        out_specs=jax.tree.map(lambda _: VMEM, outs),
        scratch_shapes=scratch,
        compiler_params=pltpu.CompilerParams(vmem_limit_bytes=limit * 2**20),
        cost_estimate=pl.CostEstimate(flops=flops, bytes_accessed=moved, transcendentals=0),
    )


def rows_of(ref, j, part):
    rows, parts, blocks, lanes = ref.shape
    flat = ref.reshape(rows * parts * blocks, lanes)
    return flat, pl.ds(part * blocks + j, rows, stride=parts * blocks)


def start_kernel(flags_ref, residual_hbm, *refs):
    given = (len(refs) - 5) // 2
    sources, loaded = refs[:given], refs[given : 2 * given]
    scaled_ref, keep_ref, send_ref, residual_ref, sems = refs[2 * given :]
    modes_ref, maps_ref = loaded[:2]
    copies = [
        pltpu.make_async_copy(source, target, sems.at[i])
        for i, (source, target) in enumerate(zip((residual_hbm,) + sources, (residual_ref,) + loaded))
    ]
    for copy in copies:
        copy.start()
    is_even, is_edge, is_upper = (flags_ref[i] > 0 for i in range(3))
    per, _, loads = scaled_ref.shape
    lanes = residual_ref.shape[-1]
    total = jnp.zeros((modes_ref.shape[1], loads), F32)
    copies[0].wait()
    copies[1].wait()
    for j in range(per):
        is_far = is_even if j == 0 else jnp.logical_not(is_even)
        scale = jnp.where(is_edge & is_far, 1.0, 0.5).astype(F32)
        for part in range(loads // lanes):
            flat, rows = rows_of(residual_ref, j, part)
            scaled_ref[j, :, part * lanes : (part + 1) * lanes] = (flat[rows, :] * scale).astype(BF)
        total += bdot(modes_ref[j], scaled_ref[j])
    copies[2].wait()
    mapped = tdot(maps_ref[0], total)
    for i, values in enumerate((total, mapped)):
        low, high = values[:, : loads // 2], values[:, loads // 2 :]
        keep_ref[i] = jnp.where(is_upper, high, low)
        send_ref[i] = jnp.where(is_upper, low, high)
    for copy in copies[3:]:
        copy.wait()


def local_kernel(flags_ref, scaled_ref, inverse_hbm, modes_ref, near_ref, far_ref, near_out, far_out, inverse_ref, sem):
    copy = pltpu.make_async_copy(inverse_hbm, inverse_ref, sem)
    copy.start()
    loads = scaled_ref.shape[-1]
    is_even = flags_ref[0] > 0
    low_modes, high_modes = (modes_ref[j].T for j in range(2))
    near_out[:, loads:] = jnp.where(is_even, high_modes, low_modes)
    far_out[:, loads:] = jnp.where(is_even, low_modes, high_modes)
    copy.wait()
    inverse = inverse_ref[...]
    low, high = (bdot(inverse[:, j, :], scaled_ref[j]) for j in range(2))
    near, far = jnp.where(is_even, high, low), jnp.where(is_even, low, high)
    near_ref[...] = near
    far_ref[...] = far
    near_out[:, :loads] = near.astype(BF)
    far_out[:, :loads] = far.astype(BF)


def pair_kernel(keep_ref, got_ref, same_ref, cross_ref, map_ref, coarse_ref, pair_ref, own_ref, sent_ref, pack_ref):
    coarse = keep_ref[0] + got_ref[0]
    for i in range(same_ref.shape[0]):
        coarse += same_ref[i].astype(F32)
    pair = tdot(map_ref[0], coarse)
    for i in range(cross_ref.shape[0]):
        pair += cross_ref[i].astype(F32)
    own = tdot(map_ref[1], pair)
    coarse_ref[...] = coarse
    pair_ref[...] = pair
    own_ref[...] = own
    sent_ref[...] = own.astype(BF)
    columns = coarse.shape[-1]
    pack_ref[:, :columns] = coarse.astype(BF)
    pack_ref[:, columns:] = map_ref[0].astype(BF)


def level_kernel(level, own_ref, got_ref, map_ref, value_ref, next_ref, sent_ref):
    value = own_ref[...] + got_ref[...].astype(F32)
    value_ref[...] = value
    following = tdot(map_ref[level], value)
    next_ref[...] = following
    sent_ref[...] = following.astype(BF)


def down_kernel(own_ref, got_ref, pack_ref, map_ref, root_ref, coarse_ref, *refs):
    values, fields_ref = refs[:-1], refs[-1]
    field = dot(root_ref[...], own_ref[...] + got_ref[...].astype(F32))
    for level in reversed(range(1, map_ref.shape[0])):
        field = dot(map_ref[level], field) + values[level - 1][...]
    fields_ref[0] = (dot(map_ref[0], field) + coarse_ref[...]).astype(BF)
    columns = field.shape[-1]
    sibling_map = pack_ref[:, columns:].astype(F32)
    fields_ref[1] = (dot(sibling_map, field) + pack_ref[:, :columns].astype(F32)).astype(BF)


def face_kernel(flags_ref, fields_ref, near_ref, far_ref, near_in_ref, far_in_ref, near_fix_ref, far_fix_ref, near_out, far_out, near_bf, mine_bf):
    loads = near_fix_ref.shape[-1]
    field = fields_ref[0]
    scale = jnp.where(flags_ref[1] > 0, 1.0, 0.5).astype(F32)
    far = (far_fix_ref[...] + bdot(far_ref[:, loads:], field)) * scale
    far_out[...] = far
    mine_bf[0] = far.astype(BF)
    own = near_fix_ref[...] + bdot(near_ref[:, loads:], field)
    other = near_in_ref[:, :loads].astype(F32) + bdot(near_in_ref[:, loads:], fields_ref[1])
    near = 0.5 * own + 0.5 * other
    near_out[...] = near
    near_bf[...] = near.astype(BF)
    mine_bf[1] = near.astype(BF)
    for i in range(far_in_ref.shape[0]):
        block = far_in_ref[i, :, :loads].astype(F32) + bdot(far_in_ref[i, :, loads:], field)
        mine_bf[2 + i] = (block * scale).astype(BF)


def gather_products(slots_ref, first, matrix_ref, sources, values_ref, list_ref, total):
    start = 0
    for source in sources:
        values_ref[start : start + source.shape[0]] = source[...]
        start += source.shape[0]
    values_ref[start] = jnp.zeros(values_ref.shape[1:], BF)
    number = matrix_ref.shape[0]
    width = 4
    for i in range(number):
        list_ref[0, i], list_ref[1, i] = 0, start

    def note(k, found):
        slot = slots_ref[k] - first
        is_here = (slot >= 0) & (slot < start)

        @pl.when(is_here)
        def _():
            list_ref[0, found], list_ref[1, found] = k, slot

        return found + is_here.astype(jnp.int32)

    found = lax.fori_loop(0, number, note, 0)

    def add(step, carry):
        products = None
        for i in range(width):
            at = step * width + i
            one = bdot(matrix_ref[list_ref[0, at]], values_ref[list_ref[1, at]])
            products = one if products is None else products + one
        total[...] += products
        return carry

    lax.fori_loop(0, (found + width - 1) // width, add, 0)


def couple_kernel(slots_ref, flags_ref, matrix_ref, inverse_ref, mine_ref, core_ref, total_ref, picked_ref, values_ref, list_ref):
    @pl.when(flags_ref[1] > 0)
    def _():
        inverse = inverse_ref[...]
        picked_ref[...] = jnp.where(flags_ref[0] > 0, inverse[:, 0, :], inverse[:, 1, :])
        total_ref[...] = jnp.zeros(total_ref.shape, F32)
        gather_products(slots_ref, 0, matrix_ref, (mine_ref, core_ref), values_ref, list_ref, total_ref)


def finish_kernel(slots_ref, flags_ref, first, matrix_ref, picked_ref, total_ref, late_ref, late_core_ref, far_ref, far_in_ref, near_ref, out_ref, sum_ref, values_ref, list_ref):
    is_even = flags_ref[0] > 0
    is_edge = flags_ref[1] > 0

    @pl.when(is_edge)
    def _():
        sum_ref[...] = total_ref[...]
        gather_products(slots_ref, first, matrix_ref, (late_ref, late_core_ref), values_ref, list_ref, sum_ref)
        sum_ref[...] = far_ref[...] - bdot(picked_ref[...], sum_ref[...].astype(BF))

    @pl.when(jnp.logical_not(is_edge))
    def _():
        sum_ref[...] = far_ref[...] + far_in_ref[...].astype(F32)

    _, parts, _, lanes = out_ref.shape
    for part in range(parts):
        columns = slice(part * lanes, (part + 1) * lanes)
        far, near = sum_ref[:, columns], near_ref[:, columns]
        for j, values in enumerate((jnp.where(is_even, far, near), jnp.where(is_even, near, far))):
            flat, rows = rows_of(out_ref, j, part)
            flat[rows, :] = values


def after(x, *others):
    return lax.optimization_barrier((x,) + others)[0]


def shards(subs, blks, residual, stiffness, pattern, neumann_inv, dirichlet_inv, basis, node_ops, root_inv):
    here = lax.axis_index("sub")
    mine = lax.axis_index("blk")
    _, per, block, loads = residual.shape
    width = basis.shape[-1]
    coupled = pattern.shape[-1]
    levels = node_ops.shape[1]
    lanes = 128
    parts = loads // lanes
    assert per == 2 and levels > 2
    even = here % 2 == 0
    edge = (here == 0) | (here == subs - 1)
    upper = mine % 2 == 1
    flags = jnp.stack([even, edge, upper]).astype(jnp.int32)
    go = functools.partial(route, subs=subs, blks=blks)
    others = range(2, blks, 2)
    shape = jax.ShapeDtypeStruct
    half_shape = width, loads // 2
    small = 2 * width * width * loads // 2
    large = 10**11

    def swap(x, sub=0, blk=0):
        return go(x, target=lambda s, b: (s ^ sub, b ^ blk))

    def turned(x):
        return jnp.transpose(x[0], (1, 0, 2))

    modes = jnp.transpose(basis[0], (0, 2, 1))
    laid = jnp.transpose(residual[0].reshape(per, block, parts, lanes), (1, 2, 0, 3))

    given = modes, node_ops[0]
    modes, maps, scaled, keep, sent = call(
        start_kernel,
        tuple(shape(x.shape, x.dtype) for x in given)
        + (shape((per, block, loads), BF),)
        + (shape((2,) + half_shape, F32),) * 2,
        [SMEM] + [HBM] * (1 + len(given)),
        2 * per * block * width * loads,
        0,
        [pltpu.VMEM(laid.shape, F32), pltpu.SemaphoreType.DMA((1 + len(given),))],
        52,
    )(flags, laid, *given)
    got = swap(sent, blk=1)
    neumann = turned(neumann_inv)
    near_fix, far_fix, to_sibling, to_far = call(
        local_kernel,
        (shape((block, loads), F32),) * 2 + (shape((block, loads + width), BF),) * 2,
        [SMEM, VMEM, HBM, VMEM],
        large,
        0,
        [pltpu.VMEM(neumann.shape, BF), pltpu.SemaphoreType.DMA(())],
        16,
    )(flags, after(scaled, got), neumann, modes)
    half_bf, mapped_bf = (keep[0] + got[0]).astype(BF), (keep[1] + got[1]).astype(BF)

    same = jnp.stack([swap(half_bf, blk=d) for d in others])
    cross = jnp.stack([swap(mapped_bf, sub=1, blk=d) for d in (0,) + tuple(others)])
    coarse, value, own, own_bf, pack = call(
        pair_kernel,
        (shape(half_shape, F32),) * 3
        + (shape(half_shape, BF), shape((width, loads // 2 + width), BF)),
        [VMEM] * 5,
        3 * small,
        8 * width * width,
    )(keep, got, same, cross, maps)
    to_sibling, to_far = after(to_sibling, own_bf), after(to_far, own_bf)
    from_sibling = swap(to_sibling, sub=1)
    from_others = jnp.stack([swap(to_far, blk=d) for d in others])
    pack = swap(pack, sub=1)
    values = [value]
    for level in range(2, levels):
        value, own, own_bf = call(
            functools.partial(level_kernel, level),
            (shape(half_shape, F32),) * 2 + (shape(half_shape, BF),),
            [VMEM] * 3,
            small,
            4 * width * width,
        )(own, swap(own_bf, sub=2 ** (level - 1)), maps)
        values.append(value)
    fields = call(
        down_kernel,
        shape((2,) + half_shape, BF),
        [VMEM] * (6 + len(values)),
        (levels + 3) * small,
        4 * (levels + 2) * width * width,
    )(own, swap(own_bf, sub=subs // 2), pack, maps, root_inv, coarse, *values)
    far_id = jnp.where(even, 0, per - 1)
    matrix = lax.dynamic_index_in_dim(stiffness[0], after(far_id, own_bf), 0, False)
    fields, from_sibling, from_others, matrix = lax.optimization_barrier(
        (fields, from_sibling, from_others, matrix)
    )
    across = swap(fields, blk=1)
    fields = jnp.concatenate(
        [jnp.where(upper, across, fields), jnp.where(upper, fields, across)], axis=2
    )

    count = 2 + len(others)
    near, far, near_bf, mine_bf = call(
        face_kernel,
        (shape((block, loads), F32),) * 2
        + (shape((block, loads), BF), shape((count, block, loads), BF)),
        [SMEM] + [VMEM] * 7,
        2 * (count + 1) * block * width * loads,
        count * block * loads * 8,
    )(flags, fields, to_sibling, to_far, from_sibling, from_others, near_fix, far_fix)

    late = jnp.stack([swap(near_bf, blk=d) for d in others])
    core = swap(mine_bf, blk=1)
    far_in = go(
        after(mine_bf[0], core),
        target=lambda s, b: (s - 1 if s % 2 == 0 else s + 1, b),
    )
    columns = pattern[0, far_id]
    offset = (columns // per) ^ mine
    is_near = columns % per != far_id
    distant = offset // 2
    slots = jnp.where(
        is_near & (distant > 0),
        2 * count + (offset % 2) * len(others) + distant - 1,
        (offset % 2) * count + jnp.where(is_near, 1, jnp.where(distant > 0, 1 + distant, 0)),
    )
    first = 2 * count
    more = 2 * len(others)
    lists = pltpu.SMEM((2, -(-coupled // 4) * 4), jnp.int32)
    total, picked = call(
        couple_kernel,
        (shape((block, loads), F32), shape((block, block), BF)),
        [SMEM, SMEM] + [VMEM] * 4,
        large,
        2 * coupled * block * block,
        [pltpu.VMEM((first + 1, block, loads), BF), lists],
    )(slots, flags, matrix, turned(dirichlet_inv), mine_bf, core)
    late, total = lax.optimization_barrier((late, total))
    late_core = swap(late, blk=1)
    result = call(
        lambda slots_ref, flags_ref, *refs: finish_kernel(slots_ref, flags_ref, first, *refs),
        shape((block, parts, per, lanes), F32),
        [SMEM, SMEM] + [VMEM] * 8,
        2 * block * block * loads,
        block * loads * 16,
        [
            pltpu.VMEM((block, loads), F32),
            pltpu.VMEM((more + 1, block, loads), BF),
            lists,
        ],
    )(slots, flags, matrix, picked, total, late, late_core, far, far_in, near)
    return jnp.transpose(result, (2, 0, 1, 3)).reshape(per, block, loads)[None]


def solution(mesh):
    placed = (
        P("sub", "blk", None, None),
        P("sub", "blk", None, None, None),
        P("sub", "blk", None),
        P("sub", "blk", None, None),
        P("sub", "blk", None, None),
        P("sub", "blk", None, None),
        P("sub", None, None, None),
        P(),
    )
    return jax.shard_map(
        functools.partial(shards, mesh.shape["sub"], mesh.shape["blk"]),
        mesh=mesh,
        in_specs=placed,
        out_specs=P("sub", "blk", None, None),
        check_vma=False,
    )
```

time: 71.4 us -> 46 us (0.64)
  local copies, waits for them, and re-layouts: 20.2 us -> 7.85 us
  Pallas kernels: 3.35 us -> 14 us
  waiting for transfers between devices: 18.7 us -> 8.88 us
  matrix products: 6.86 us -> 0 us
  starting transfers between devices: 18.7 us -> 14.2 us
  other arithmetic: 3.02 us -> 0.18 us
    pallas_call x2 -> x8, Pallas kernels: 3.35 us -> 14 us  [the longest x1 3.28 us: shards(): call(couple_kernel, (shape((block, loads), F32), shape((block, block), BF...]
    ppermute x16 -> x14, waiting for transfers between devices: 18.7 us -> 8.88 us  [route(): return lax.ppermute(x, ('sub', 'blk'), pairs)]
    dynamic_slice x3 -> x2, local copies, waits for them, and re-layouts: 11 us -> 3.79 us  [shards(): lax.dynamic_index_in_dim(stiffness[0], after(far_id, own_bf), 0, False)]
    dot_general x12 -> x0, matrix products: 6.86 us -> none  [the longest x5 3.62 us: tdot(): lax.dot_general(a, b, (((0,), (0,)), ((), ())), precision=HIGHEST, prefer...]
    ppermute x16 -> x14, starting transfers between devices: 18.7 us -> 14.2 us  [route(): return lax.ppermute(x, ('sub', 'blk'), pairs)]
    squeeze x2 -> x0, local copies, waits for them, and re-layouts: 2.5 us -> none  [the longest x1 1.8 us: shards(): field = dot(maps[level], field) + values[level]]
    convert_element_type x3 -> x2, other arithmetic: 1.55 us -> 0.1 us  [the longest x1 0.08 us: shards(): flags = jnp.stack([even, edge, upper]).astype(jnp.int32)]
    select_n x4 -> x1, other arithmetic: 1.38 us -> 0.03 us  [shards(): jnp.where(is_near & (distant > 0), 2 * count + offset % 2 * len(others) +...]
  transfers between devices with their start and end apart: 16 -> 14, of which waited for: 6 -> 8; matrix products, arithmetic and copies ran while one was open for 32% -> 9% of each run, Pallas kernels for 0% -> 15%
where the time goes in v3:
time: 46 us; the launch traced here: 45.2 us
  starting transfers between devices  14.2 us (31%)
  Pallas kernels  14 us (30%)
  waiting for transfers between devices  8.88 us (19%)
  local copies, waits for them, and re-layouts  7.85 us (17%)
    ppermute x14, starting transfers between devices, route(): return lax.ppermute(x, ('sub', 'blk'), pairs)  14.2 us
    ppermute x14, waiting for transfers between devices, route(): return lax.ppermute(x, ('sub', 'blk'), pairs)  8.88 us
    unnamed x16, local copies, waits for them, and re-layouts  4.05 us
    dynamic_slice x2, local copies, waits for them, and re-layouts, shards(): lax.dynamic_index_in_dim(stiffness[0], after(far_id, own_bf), 0, False)  3.79 us
    pallas_call x1, Pallas kernels, shards(): call(couple_kernel, (shape((block, loads), F32), shape((block, block), BF...  3.28 us
    pallas_call x1, Pallas kernels, shards(): call(lambda slots_ref, flags_ref, *refs: finish_kernel(slots_ref, flags_r...  2.59 us
    pallas_call x1, Pallas kernels, shards(): call(start_kernel, tuple((shape(x.shape, x.dtype) for x in given)) + (sha...  2.39 us
    pallas_call x1, Pallas kernels, shards(): call(local_kernel, (shape((block, loads), F32),) * 2 + (shape((block, loa...  2.25 us
  transfers between devices with their start and end apart: 14, of which 8 were waited for; matrix products, arithmetic and copies ran while one was open for 9% of the time, Pallas kernels for 15%

profile of v3, /device:TPU:0, one launch (start us, length us, event | category | flops | bytes accessed | tf_op | source)
XLA Modules:
  0.0 45.2 jit_solution(2813542046010424665)
XLA Ops:
  0.1 1.0 %copy-done = bf16[1,2,375,192]{2,3,1,0:T(8,128)(2,1)S(1)} copy-done((bf16[1,2,375,192]{2,3,1,0:T(8,128)(2,1)S(1)}, bf16[1,2,375,192]{2,3,1,0:T(8,128)(2,1)}, u32[]{:S(2)}) %copy-start) | copy-done | bytes 288024
  1.0 2.4 %shard_map.82 = (bf16[2,192,375]{2,1,0:T(8,128)(2,1)S(1)}, f32[3,192,192]{2,1,0:T(8,128)S(1)}, bf16[2,375,256]{2,1,0:T(8,128)(2,1)S(1)}, f32[2,192,128]{2,1,0:T(8,128)S(1)}, f32[2,192,128]{2,1,0:T(8,128)S(1)}) custom-call(s32[3]{0:T(128)S(1)} %add_convert_fusion.flags_ref, f32[375,2,2,128]{3,2,1,0:T(2,128)} %bitcast.55, bf16[2,192,375]{2,1,0:T(8,128)(2,1)S(1)} %bitcast.49, ...), custom_call_target="tpu_custom_call" | custom-call | flops 73728000 | tf_op jit(solution)/shard_map/pallas_call | solution.py:274
  4.0 1.1 %collective-permute-done.got_ref = f32[2,192,128]{2,1,0:T(8,128)S(1)} collective-permute-done((f32[2,192,128]{2,1,0:T(8,128)S(1)}, f32[2,192,128]{2,1,0:T(8,128)S(1)}, u32[]{:S(2)}, u32[]{:S(2)}) %collective-permute-start) | collective-permute-done | bytes 196640 | tf_op jit(solution)/shard_map/ppermute | solution.py:24
  5.1 2.9 %collective-permute-start.2 = (bf16[192,128]{1,0:T(8,128)(2,1)S(1)}, bf16[192,128]{1,0:T(8,128)(2,1)S(1)}, u32[]{:S(2)}, u32[]{:S(2)}) collective-permute-start(bf16[192,128]{1,0:T(8,128)(2,1)S(1)} %get-tuple-element.73), channel_id=1, source_target_pairs={{0,4},{1,5},{2,6},{3,7},{4,0},{5,1},{6,2},{7,3},{8,12},{9,13},{10,... | collective-permute-start | bytes 147464 | tf_op jit(solution)/shard_map/ppermute | solution.py:24
  8.0 1.5 %collective-permute-start.3 = (bf16[192,128]{1,0:T(8,128)(2,1)S(1)}, bf16[192,128]{1,0:T(8,128)(2,1)S(1)}, u32[]{:S(2)}, u32[]{:S(2)}) collective-permute-start(bf16[192,128]{1,0:T(8,128)(2,1)S(1)} %get-tuple-element.73), channel_id=1, source_target_pairs={{0,6},{1,7},{2,4},{3,5},{4,2},{5,3},{6,0},{7,1},{8,14},{9,15},{10,... | collective-permute-start | bytes 147464 | tf_op jit(solution)/shard_map/ppermute | solution.py:24
  9.5 1.1 %copy-done.4 = bf16[1,2,375,375]{3,1,2,0:T(2,128)(2,1)S(1)} copy-done((bf16[1,2,375,375]{3,1,2,0:T(2,128)(2,1)S(1)}, bf16[1,2,375,375]{3,1,2,0:T(2,128)(2,1)}, u32[]{:S(2)}) %copy-start.4) | copy-done | bytes 562524
  10.6 2.2 %shard_map.86 = (f32[375,256]{1,0:T(8,128)S(1)}, f32[375,256]{1,0:T(8,128)S(1)}, bf16[375,448]{1,0:T(8,128)(2,1)S(1)}, bf16[375,448]{1,0:T(8,128)(2,1)S(1)}) custom-call(s32[3]{0:T(128)S(1)} %add_convert_fusion.flags_ref, bf16[2,375,256]{2,1,0:T(8,128)(2,1)S(1)} %get-tuple-element.51.scaled_ref, bf16[375,2,375]{2,1,0:T(2,128)(2,1)S(1)} %bitcast.53, ...), custom_call_target="tpu_custom_call" | custom-call | flops 99999997952 | tf_op jit(solution)/shard_map/pallas_call | solution.py:287
  13.6 1.1 %shard_map.83 = (f32[192,128]{1,0:T(8,128)S(1)}, f32[192,128]{1,0:T(8,128)S(1)}, f32[192,128]{1,0:T(8,128)S(1)}, bf16[192,128]{1,0:T(8,128)(2,1)S(1)}, bf16[192,320]{1,0:T(8,128)(2,1)}) custom-call(f32[2,192,128]{2,1,0:T(8,128)S(1)} %get-tuple-element.39.keep_ref, f32[2,192,128]{2,1,0:T(8,128)S(1)} %collective-permute-done.got_ref, ...), custom_call_target="tpu_custom_call" | custom-call | flops 28311552 | bytes 294912 | tf_op jit(solution)/shard_map/pallas_call | solution.py:300
  14.7 1.3 %collective-permute-start.8 = (bf16[375,448]{1,0:T(8,128)(2,1)S(1)}, bf16[375,448]{1,0:T(8,128)(2,1)S(1)}, u32[]{:S(2)}, u32[]{:S(2)}) collective-permute-start(bf16[375,448]{1,0:T(8,128)(2,1)S(1)} %get-tuple-element.56.far_ref), channel_id=1, source_target_pairs={{0,2},{1,3},{2,0},{3,1},{4,6},{5,7},{6,4},{7,5},{8,10},{9,11},{10,... | collective-permute-start | bytes 1008008 | tf_op jit(solution)/shard_map/ppermute | solution.py:24
  16.0 1.5 %collective-permute-start.7 = (bf16[375,448]{1,0:T(8,128)(2,1)S(1)}, bf16[375,448]{1,0:T(8,128)(2,1)S(1)}, u32[]{:S(2)}, u32[]{:S(2)}) collective-permute-start(bf16[375,448]{1,0:T(8,128)(2,1)S(1)} %get-tuple-element.54.near_ref), channel_id=1, source_target_pairs={{0,4},{1,5},{2,6},{3,7},{4,0},{5,1},{6,2},{7,3},{8,12},{9,13},{10,... | collective-permute-start | bytes 1008008 | tf_op jit(solution)/shard_map/ppermute | solution.py:24
  17.5 1.6 %collective-permute-start.4 = (bf16[192,128]{1,0:T(8,128)(2,1)S(1)}, bf16[192,128]{1,0:T(8,128)(2,1)S(1)}, u32[]{:S(2)}, u32[]{:S(2)}) collective-permute-start(bf16[192,128]{1,0:T(8,128)(2,1)S(1)} %get-tuple-element.43), channel_id=1, source_target_pairs={{0,8},{1,9},{2,10},{3,11},{4,12},{5,13},{6,14},{7,15},{8,0},{9,1},... | collective-permute-start | bytes 147464 | tf_op jit(solution)/shard_map/ppermute | solution.py:24
  19.6 2.0 %collective-permute-done.4.got_ref = bf16[192,128]{1,0:T(8,128)(2,1)S(1)} collective-permute-done((bf16[192,128]{1,0:T(8,128)(2,1)S(1)}, bf16[192,128]{1,0:T(8,128)(2,1)S(1)}, u32[]{:S(2)}, u32[]{:S(2)}) %collective-permute-start.4) | collective-permute-done | bytes 49184 | tf_op jit(solution)/shard_map/ppermute | solution.py:24
  22.2 0.8 %copy-done.3 = bf16[192,128]{1,0:T(8,128)(2,1)S(1)} copy-done((bf16[192,128]{1,0:T(8,128)(2,1)S(1)}, bf16[192,128]{1,0:T(8,128)(2,1)}, u32[]{:S(2)}) %copy-start.3) | copy-done | bytes 49176
  23.9 2.6 %collective-permute-start.5 = (bf16[192,128]{1,0:T(8,128)(2,1)}, bf16[192,128]{1,0:T(8,128)(2,1)S(1)}, u32[]{:S(2)}, u32[]{:S(2)}) collective-permute-start(bf16[192,128]{1,0:T(8,128)(2,1)} %copy-done.6), channel_id=1, source_target_pairs={{0,16},{1,17},{2,18},{3,19},{4,20},{5,21},{6,22},{7,23},{8,24},{9,... | collective-permute-start | bytes 147464 | tf_op jit(solution)/shard_map/ppermute | solution.py:24
  26.5 2.8 %constant_dynamic-slice_fusion = bf16[1,1,16,375,375]{4,2,3,1,0:T(8,128)(2,1)S(1)} fusion(bf16[1,2,16,375,375]{4,2,3,1,0:T(8,128)(2,1)} %param.9, s32[]{:T(128)S(6)} %select_n.73), kind=kLoop, calls=%fused_computation.28 | loop fusion | bytes 9000004 | tf_op jit(solution)/shard_map/jit(dynamic_index_in_dim)/dynamic_slice | solution.py:330
  29.3 1.0 %copy.11 = bf16[1,1,16,375,375]{4,3,2,1,0:T(8,128)(2,1)S(1)} copy(bf16[1,1,16,375,375]{4,2,3,1,0:T(8,128)(2,1)S(1)} %constant_dynamic-slice_fusion) | data formatting | bytes 9000000 | tf_op jit(solution)/shard_map/jit(dynamic_index_in_dim)/dynamic_slice | solution.py:330
  30.4 1.1 %shard_map.85 = bf16[2,192,128]{2,1,0:T(8,128)(2,1)S(1)} custom-call(f32[192,128]{1,0:T(8,128)S(1)} %get-tuple-element.44.own_ref, bf16[192,128]{1,0:T(8,128)(2,1)S(1)} %collective-permute-done.5.got_ref, bf16[192,320]{1,0:T(8,128)(2,1)S(1)} %collective-permute-done.6.pack_ref, f32[3,192,192]{2,1,0:T(8,128)S(1)} %get-tuple-element.41.map_ref, ...), custom_call_target="tpu_custom_call" | custom-call | flops 56623104 | bytes 737280 | tf_op jit(solution)/shard_map/pallas_call | solution.py:322
  31.5 1.3 %collective-permute-done.9 = bf16[2,192,128]{2,1,0:T(8,128)(2,1)S(1)} collective-permute-done((bf16[2,192,128]{2,1,0:T(8,128)(2,1)S(1)}, bf16[2,192,128]{2,1,0:T(8,128)(2,1)S(1)}, u32[]{:S(2)}, u32[]{:S(2)}) %collective-permute-start.9) | collective-permute-done | bytes 98336 | tf_op jit(solution)/shard_map/ppermute | solution.py:24
  32.9 0.9 %shard_map.87 = (f32[375,256]{1,0:T(8,128)S(1)}, f32[375,256]{1,0:T(8,128)S(1)}, bf16[375,256]{1,0:T(8,128)(2,1)S(1)}, bf16[3,375,256]{2,1,0:T(8,128)(2,1)S(1)}) custom-call(s32[3]{0:T(128)S(1)} %add_convert_fusion.flags_ref, bf16[2,192,256]{2,1,0:T(8,128)(2,1)S(1)} %pad_maximum_fusion.fields_ref, bf16[375,448]{1,0:T(8,128)(2,1)S(1)} %get-tuple-element.54.near_ref, ...), custom_call_target="tpu_custom_call" | custom-call | flops 147456000 | bytes 2304000 | tf_op jit(solution)/shard_map/pallas_call | solution.py:340
  34.9 1.0 %collective-permute-done.10.core_ref = bf16[3,375,256]{2,1,0:T(8,128)(2,1)S(1)} collective-permute-done((bf16[3,375,256]{2,1,0:T(8,128)(2,1)S(1)}, bf16[3,375,256]{2,1,0:T(8,128)(2,1)S(1)}, u32[]{:S(2)}, u32[]{:S(2)}) %collective-permute-start.10) | collective-permute-done | bytes 576032 | tf_op jit(solution)/shard_map/ppermute | solution.py:24
  36.6 3.3 %shard_map.88 = (f32[375,256]{1,0:T(8,128)S(1)}, bf16[375,375]{1,0:T(8,128)(2,1)S(1)}) custom-call(s32[16]{0:T(128)S(1)} %and_select_fusion.1.slots_ref, s32[3]{0:T(128)S(1)} %add_convert_fusion.flags_ref, bf16[16,375,375]{2,1,0:T(8,128)(2,1)S(1)} %bitcast.46, bf16[375,2,375]{2,1,0:T(2,128)(2,1)S(1)} %bitcast.54, ...), custom_call_target="tpu_custom_call" | custom-call | flops 99999997952 | bytes 4500000 | tf_op jit(solution)/shard_map/pallas_call | solution.py:367
  39.9 1.4 %collective-permute-done.11 = bf16[375,256]{1,0:T(8,128)(2,1)S(1)} collective-permute-done((bf16[375,256]{1,0:T(8,128)(2,1)S(1)}, bf16[375,256]{1,0:T(8,128)(2,1)S(1)}, u32[]{:S(2)}, u32[]{:S(2)}) %collective-permute-start.11) | collective-permute-done | bytes 192032 | tf_op jit(solution)/shard_map/ppermute | solution.py:24
  41.2 1.4 %collective-permute-done.12.refs_4_ = bf16[1,375,256]{2,1,0:T(8,128)(2,1)S(1)} collective-permute-done((bf16[1,375,256]{2,1,0:T(8,128)(2,1)S(1)}, bf16[1,375,256]{2,1,0:T(8,128)(2,1)S(1)}, u32[]{:S(2)}, u32[]{:S(2)}) %collective-permute-start.12) | collective-permute-done | bytes 192032 | tf_op jit(solution)/shard_map/ppermute | solution.py:24
  42.7 2.6 %shard_map.89 = f32[375,2,2,128]{3,2,1,0:T(2,128)} custom-call(s32[16]{0:T(128)S(1)} %and_select_fusion.1.slots_ref, s32[3]{0:T(128)S(1)} %add_convert_fusion.flags_ref, bf16[16,375,375]{2,1,0:T(8,128)(2,1)S(1)} %bitcast.47, bf16[375,375]{1,0:T(8,128)(2,1)S(1)} %get-tuple-element.65.refs_1_, f32[375,256]{1,0:T(8,128)S(1)} %get-tuple-element.68.refs_2_, ...), custom_call_target="tpu_custom_call" | custom-call | flops 72000000 | bytes 1536000 | tf_op jit(solution)/shard_map/pallas_call | solution.py:377
  (37 shorter events, 5.3 us)
Async XLA Ops:
  0.1 1.0 %copy-start = (bf16[1,2,375,192]{2,3,1,0:T(8,128)(2,1)S(1)}, bf16[1,2,375,192]{2,3,1,0:T(8,128)(2,1)}, u32[]{:S(2)}) copy-start(bf16[1,2,375,192]{2,3,1,0:T(8,128)(2,1)} %param.13) | copy-start | bytes 864004
  3.4 1.6 %collective-permute-start = (f32[2,192,128]{2,1,0:T(8,128)S(1)}, f32[2,192,128]{2,1,0:T(8,128)S(1)}, u32[]{:S(2)}, u32[]{:S(2)}) collective-permute-start(f32[2,192,128]{2,1,0:T(8,128)S(1)} %get-tuple-element.40), channel_id=1, source_target_pairs={{0,1},{1,0},{2,3},{3,2},{4,5},{5,4},{6,7},{7,6},{8,9},{9,8},{10,11... | collective-permute-start | bytes 589832 | tf_op jit(solution)/shard_map/ppermute | solution.py:24
  5.1 7.8 %collective-permute-start.2 = (bf16[192,128]{1,0:T(8,128)(2,1)S(1)}, bf16[192,128]{1,0:T(8,128)(2,1)S(1)}, u32[]{:S(2)}, u32[]{:S(2)}) collective-permute-start(bf16[192,128]{1,0:T(8,128)(2,1)S(1)} %get-tuple-element.73), channel_id=1, source_target_pairs={{0,4},{1,5},{2,6},{3,7},{4,0},{5,1},{6,2},{7,3},{8,12},{9,13},{10,... | collective-permute-start | bytes 147464 | tf_op jit(solution)/shard_map/ppermute | solution.py:24
  8.0 5.0 %collective-permute-start.3 = (bf16[192,128]{1,0:T(8,128)(2,1)S(1)}, bf16[192,128]{1,0:T(8,128)(2,1)S(1)}, u32[]{:S(2)}, u32[]{:S(2)}) collective-permute-start(bf16[192,128]{1,0:T(8,128)(2,1)S(1)} %get-tuple-element.73), channel_id=1, source_target_pairs={{0,6},{1,7},{2,4},{3,5},{4,2},{5,3},{6,0},{7,1},{8,14},{9,15},{10,... | collective-permute-start | bytes 147464 | tf_op jit(solution)/shard_map/ppermute | solution.py:24
  9.5 4.1 %collective-permute-start.1 = (bf16[192,128]{1,0:T(8,128)(2,1)S(1)}, bf16[192,128]{1,0:T(8,128)(2,1)S(1)}, u32[]{:S(2)}, u32[]{:S(2)}) collective-permute-start(bf16[192,128]{1,0:T(8,128)(2,1)S(1)} %get-tuple-element.74), channel_id=1, source_target_pairs={{0,2},{1,3},{2,0},{3,1},{4,6},{5,7},{6,4},{7,5},{8,10},{9,11},{10,... | collective-permute-start | bytes 147464 | tf_op jit(solution)/shard_map/ppermute | solution.py:24
  9.5 1.1 %copy-start.4 = (bf16[1,2,375,375]{3,1,2,0:T(2,128)(2,1)S(1)}, bf16[1,2,375,375]{3,1,2,0:T(2,128)(2,1)}, u32[]{:S(2)}) copy-start(bf16[1,2,375,375]{3,1,2,0:T(2,128)(2,1)} %param.11) | copy-start | bytes 1687504
  14.7 16.7 %collective-permute-start.8 = (bf16[375,448]{1,0:T(8,128)(2,1)S(1)}, bf16[375,448]{1,0:T(8,128)(2,1)S(1)}, u32[]{:S(2)}, u32[]{:S(2)}) collective-permute-start(bf16[375,448]{1,0:T(8,128)(2,1)S(1)} %get-tuple-element.56.far_ref), channel_id=1, source_target_pairs={{0,2},{1,3},{2,0},{3,1},{4,6},{5,7},{6,4},{7,5},{8,10},{9,11},{10,... | collective-permute-start | bytes 1008008 | tf_op jit(solution)/shard_map/ppermute | solution.py:24
  16.0 15.5 %collective-permute-start.7 = (bf16[375,448]{1,0:T(8,128)(2,1)S(1)}, bf16[375,448]{1,0:T(8,128)(2,1)S(1)}, u32[]{:S(2)}, u32[]{:S(2)}) collective-permute-start(bf16[375,448]{1,0:T(8,128)(2,1)S(1)} %get-tuple-element.54.near_ref), channel_id=1, source_target_pairs={{0,4},{1,5},{2,6},{3,7},{4,0},{5,1},{6,2},{7,3},{8,12},{9,13},{10,... | collective-permute-start | bytes 1008008 | tf_op jit(solution)/shard_map/ppermute | solution.py:24
  17.5 4.1 %collective-permute-start.4 = (bf16[192,128]{1,0:T(8,128)(2,1)S(1)}, bf16[192,128]{1,0:T(8,128)(2,1)S(1)}, u32[]{:S(2)}, u32[]{:S(2)}) collective-permute-start(bf16[192,128]{1,0:T(8,128)(2,1)S(1)} %get-tuple-element.43), channel_id=1, source_target_pairs={{0,8},{1,9},{2,10},{3,11},{4,12},{5,13},{6,14},{7,15},{8,0},{9,1},... | collective-permute-start | bytes 147464 | tf_op jit(solution)/shard_map/ppermute | solution.py:24
  19.1 11.3 %collective-permute-start.6 = (bf16[192,320]{1,0:T(8,128)(2,1)}, bf16[192,320]{1,0:T(8,128)(2,1)S(1)}, u32[]{:S(2)}, u32[]{:S(2)}) collective-permute-start(bf16[192,320]{1,0:T(8,128)(2,1)} %get-tuple-element.46), channel_id=1, source_target_pairs={{0,4},{1,5},{2,6},{3,7},{4,0},{5,1},{6,2},{7,3},{8,12},{9,13},{10,... | collective-permute-start | bytes 368648 | tf_op jit(solution)/shard_map/ppermute | solution.py:24
  21.6 0.6 %copy-start.2 = (bf16[192,128]{1,0:T(8,128)(2,1)}, bf16[192,128]{1,0:T(8,128)(2,1)S(1)}, u32[]{:S(2)}) copy-start(bf16[192,128]{1,0:T(8,128)(2,1)S(1)} %collective-permute-done.4.got_ref) | copy-start | bytes 147460
  22.2 0.8 %copy-start.3 = (bf16[192,128]{1,0:T(8,128)(2,1)S(1)}, bf16[192,128]{1,0:T(8,128)(2,1)}, u32[]{:S(2)}) copy-start(bf16[192,128]{1,0:T(8,128)(2,1)} %copy-done.2) | copy-start | bytes 147460
  23.3 0.6 %copy-start.6 = (bf16[192,128]{1,0:T(8,128)(2,1)}, bf16[192,128]{1,0:T(8,128)(2,1)S(1)}, u32[]{:S(2)}) copy-start(bf16[192,128]{1,0:T(8,128)(2,1)S(1)} %get-tuple-element.45) | copy-start | bytes 147460
  23.9 6.4 %collective-permute-start.5 = (bf16[192,128]{1,0:T(8,128)(2,1)}, bf16[192,128]{1,0:T(8,128)(2,1)S(1)}, u32[]{:S(2)}, u32[]{:S(2)}) collective-permute-start(bf16[192,128]{1,0:T(8,128)(2,1)} %copy-done.6), channel_id=1, source_target_pairs={{0,16},{1,17},{2,18},{3,19},{4,20},{5,21},{6,22},{7,23},{8,24},{9,... | collective-permute-start | bytes 147464 | tf_op jit(solution)/shard_map/ppermute | solution.py:24
  29.3 1.1 %copy-start.1 = (f32[192,192]{1,0:T(8,128)S(1)}, f32[192,192]{1,0:T(8,128)}, u32[]{:S(2)}) copy-start(f32[192,192]{1,0:T(8,128)} %root_ref.1) | copy-start | bytes 442372
  30.3 3.8 %copy-start.7 = (s32[1,2,16]{2,1,0:T(2,128)S(1)}, s32[1,2,16]{2,1,0:T(2,128)}, u32[]{:S(2)}) copy-start(s32[1,2,16]{2,1,0:T(2,128)} %param.10) | copy-start | bytes 388
  30.3 6.2 %copy-start.5 = (bf16[1,2,375,375]{3,1,2,0:T(2,128)(2,1)S(1)}, bf16[1,2,375,375]{3,1,2,0:T(2,128)(2,1)}, u32[]{:S(2)}) copy-start(bf16[1,2,375,375]{3,1,2,0:T(2,128)(2,1)} %param.12) | copy-start | bytes 1687504
  31.5 1.4 %collective-permute-start.9 = (bf16[2,192,128]{2,1,0:T(8,128)(2,1)S(1)}, bf16[2,192,128]{2,1,0:T(8,128)(2,1)S(1)}, u32[]{:S(2)}, u32[]{:S(2)}) collective-permute-start(bf16[2,192,128]{2,1,0:T(8,128)(2,1)S(1)} %shard_map.85), channel_id=1, source_target_pairs={{0,1},{1,0},{2,3},{3,2},{4,5},{5,4},{6,7},{7,6},{8,9},{9,8},{10,11... | collective-permute-start | bytes 294920 | tf_op jit(solution)/shard_map/ppermute | solution.py:24
  33.8 2.1 %collective-permute-start.10 = (bf16[3,375,256]{2,1,0:T(8,128)(2,1)S(1)}, bf16[3,375,256]{2,1,0:T(8,128)(2,1)S(1)}, u32[]{:S(2)}, u32[]{:S(2)}) collective-permute-start(bf16[3,375,256]{2,1,0:T(8,128)(2,1)S(1)} %get-tuple-element.64.mine_ref), channel_id=1, source_target_pairs={{0,1},{1,0},{2,3},{3,2},{4,5},{5,4},{6,7},{7,6},{8,9},{9,8},{10,11... | collective-permute-start | bytes 1728008 | tf_op jit(solution)/shard_map/ppermute | solution.py:24
  34.1 7.1 %collective-permute-start.11 = (bf16[375,256]{1,0:T(8,128)(2,1)S(1)}, bf16[375,256]{1,0:T(8,128)(2,1)S(1)}, u32[]{:S(2)}, u32[]{:S(2)}) collective-permute-start(bf16[375,256]{1,0:T(8,128)(2,1)S(1)} %get-tuple-element.66), channel_id=1, source_target_pairs={{0,2},{1,3},{2,0},{3,1},{4,6},{5,7},{6,4},{7,5},{8,10},{9,11},{10,... | collective-permute-start | bytes 576008 | tf_op jit(solution)/shard_map/ppermute | solution.py:24
  35.9 5.3 %collective-permute-start.13 = (bf16[375,256]{1,0:T(8,128)(2,1)S(1)}, bf16[375,256]{1,0:T(8,128)(2,1)S(1)}, u32[]{:S(2)}, u32[]{:S(2)}) collective-permute-start(bf16[375,256]{1,0:T(8,128)(2,1)S(1)} %slice_bitcast_fusion), channel_id=1, source_target_pairs={{4,8},{5,9},{6,10},{7,11},{8,4},{9,5},{10,6},{11,7},{12,16},{13,17... | collective-permute-start | bytes 576008 | tf_op jit(solution)/shard_map/ppermute | solution.py:24
  41.2 1.4 %collective-permute-start.12 = (bf16[1,375,256]{2,1,0:T(8,128)(2,1)S(1)}, bf16[1,375,256]{2,1,0:T(8,128)(2,1)S(1)}, u32[]{:S(2)}, u32[]{:S(2)}) collective-permute-start(bf16[1,375,256]{2,1,0:T(8,128)(2,1)S(1)} %bitcast.50), channel_id=1, source_target_pairs={{0,1},{1,0},{2,3},{3,2},{4,5},{5,4},{6,7},{7,6},{8,9},{9,8},{10,11... | collective-permute-start | bytes 576008 | tf_op jit(solution)/shard_map/ppermute | solution.py:24

commit v4 on v3

--- a/solution.py
+++ b/solution.py
@@ -115,7 +115,7 @@
     far_out[:, :loads] = far.astype(BF)
 
 
-def pair_kernel(keep_ref, got_ref, same_ref, cross_ref, map_ref, coarse_ref, pair_ref, own_ref, sent_ref, pack_ref):
+def pair_kernel(keep_ref, got_ref, same_ref, cross_ref, map_ref, coarse_ref, pair_ref, own_ref, sent_ref, share_ref):
     coarse = keep_ref[0] + got_ref[0]
     for i in range(same_ref.shape[0]):
         coarse += same_ref[i].astype(F32)
@@ -127,9 +127,16 @@
     pair_ref[...] = pair
     own_ref[...] = own
     sent_ref[...] = own.astype(BF)
-    columns = coarse.shape[-1]
-    pack_ref[:, :columns] = coarse.astype(BF)
-    pack_ref[:, columns:] = map_ref[0].astype(BF)
+    share_ref[...] = coarse.astype(BF)
+
+
+def offer_kernel(coarse_ref, near_ref, near_fix_ref, map_ref, out_ref):
+    loads = near_fix_ref.shape[-1]
+    modes = near_ref[:, loads:]
+    out_ref[:, :loads] = (near_fix_ref[...] + bdot(modes, coarse_ref[...])).astype(BF)
+    high = map_ref[0].astype(BF)
+    low = (map_ref[0] - high.astype(F32)).astype(BF)
+    out_ref[:, loads:] = (bdot(modes, high) + bdot(modes, low)).astype(BF)
 
 
 def level_kernel(level, own_ref, got_ref, map_ref, value_ref, next_ref, sent_ref):
@@ -140,44 +147,42 @@
     sent_ref[...] = following.astype(BF)
 
 
-def down_kernel(own_ref, got_ref, pack_ref, map_ref, root_ref, coarse_ref, *refs):
+def down_kernel(own_ref, got_ref, map_ref, root_ref, coarse_ref, *refs):
     values, fields_ref = refs[:-1], refs[-1]
     field = dot(root_ref[...], own_ref[...] + got_ref[...].astype(F32))
     for level in reversed(range(1, map_ref.shape[0])):
         field = dot(map_ref[level], field) + values[level - 1][...]
     fields_ref[0] = (dot(map_ref[0], field) + coarse_ref[...]).astype(BF)
-    columns = field.shape[-1]
-    sibling_map = pack_ref[:, columns:].astype(F32)
-    fields_ref[1] = (dot(sibling_map, field) + pack_ref[:, :columns].astype(F32)).astype(BF)
-
-
-def face_kernel(flags_ref, fields_ref, near_ref, far_ref, near_in_ref, far_in_ref, near_fix_ref, far_fix_ref, near_out, far_out, near_bf, mine_bf):
+    fields_ref[1] = field.astype(BF)
+
+
+def face_kernel(flags_ref, fields_ref, near_ref, far_ref, near_in_ref, far_in_ref, near_fix_ref, far_fix_ref, near_out, far_out, near_bf, far_bf, mine_bf):
     loads = near_fix_ref.shape[-1]
     field = fields_ref[0]
-    scale = jnp.where(flags_ref[1] > 0, 1.0, 0.5).astype(F32)
-    far = (far_fix_ref[...] + bdot(far_ref[:, loads:], field)) * scale
-    far_out[...] = far
-    mine_bf[0] = far.astype(BF)
     own = near_fix_ref[...] + bdot(near_ref[:, loads:], field)
     other = near_in_ref[:, :loads].astype(F32) + bdot(near_in_ref[:, loads:], fields_ref[1])
     near = 0.5 * own + 0.5 * other
     near_out[...] = near
     near_bf[...] = near.astype(BF)
     mine_bf[1] = near.astype(BF)
+    scale = jnp.where(flags_ref[1] > 0, 1.0, 0.5).astype(F32)
+    far = (far_fix_ref[...] + bdot(far_ref[:, loads:], field)) * scale
+    far_out[...] = far
+    far_bf[...] = far.astype(BF)
+    mine_bf[0] = far.astype(BF)
     for i in range(far_in_ref.shape[0]):
         block = far_in_ref[i, :, :loads].astype(F32) + bdot(far_in_ref[i, :, loads:], field)
         mine_bf[2 + i] = (block * scale).astype(BF)
 
 
-def gather_products(slots_ref, first, matrix_ref, sources, values_ref, list_ref, total):
+def gather_products(slots_ref, first, matrix_ref, sources, values_ref, list_ref, total, width):
     start = 0
     for source in sources:
         values_ref[start : start + source.shape[0]] = source[...]
         start += source.shape[0]
     values_ref[start] = jnp.zeros(values_ref.shape[1:], BF)
     number = matrix_ref.shape[0]
-    width = 4
-    for i in range(number):
+    for i in range(list_ref.shape[1]):
         list_ref[0, i], list_ref[1, i] = 0, start
 
     def note(k, found):
@@ -193,24 +198,25 @@
     found = lax.fori_loop(0, number, note, 0)
 
     def add(step, carry):
-        products = None
-        for i in range(width):
-            at = step * width + i
-            one = bdot(matrix_ref[list_ref[0, at]], values_ref[list_ref[1, at]])
-            products = one if products is None else products + one
-        total[...] += products
+        places = [step * width + i for i in range(width)]
+        matrices = jnp.concatenate([matrix_ref[list_ref[0, at]] for at in places], axis=1)
+        values = jnp.concatenate([values_ref[list_ref[1, at]] for at in places], axis=0)
+        total[...] += bdot(matrices, values)
         return carry
 
     lax.fori_loop(0, (found + width - 1) // width, add, 0)
 
 
-def couple_kernel(slots_ref, flags_ref, matrix_ref, inverse_ref, mine_ref, core_ref, total_ref, picked_ref, values_ref, list_ref):
+def pick_kernel(flags_ref, inverse_ref, picked_ref):
+    inverse = inverse_ref[...]
+    picked_ref[...] = jnp.where(flags_ref[0] > 0, inverse[:, 0, :], inverse[:, 1, :])
+
+
+def couple_kernel(slots_ref, flags_ref, matrix_ref, mine_ref, core_ref, total_ref, values_ref, list_ref):
     @pl.when(flags_ref[1] > 0)
     def _():
-        inverse = inverse_ref[...]
-        picked_ref[...] = jnp.where(flags_ref[0] > 0, inverse[:, 0, :], inverse[:, 1, :])
         total_ref[...] = jnp.zeros(total_ref.shape, F32)
-        gather_products(slots_ref, 0, matrix_ref, (mine_ref, core_ref), values_ref, list_ref, total_ref)
+        gather_products(slots_ref, 0, matrix_ref, (mine_ref, core_ref), values_ref, list_ref, total_ref, 8)
 
 
 def finish_kernel(slots_ref, flags_ref, first, matrix_ref, picked_ref, total_ref, late_ref, late_core_ref, far_ref, far_in_ref, near_ref, out_ref, sum_ref, values_ref, list_ref):
@@ -220,7 +226,7 @@
     @pl.when(is_edge)
     def _():
         sum_ref[...] = total_ref[...]
-        gather_products(slots_ref, first, matrix_ref, (late_ref, late_core_ref), values_ref, list_ref, sum_ref)
+        gather_products(slots_ref, first, matrix_ref, (late_ref, late_core_ref), values_ref, list_ref, sum_ref, 4)
         sum_ref[...] = far_ref[...] - bdot(picked_ref[...], sum_ref[...].astype(BF))
 
     @pl.when(jnp.logical_not(is_edge))
@@ -263,6 +269,10 @@
 
     def swap(x, sub=0, blk=0):
         return go(x, target=lambda s, b: (s ^ sub, b ^ blk))
+
+    def joined(x):
+        other = swap(x, blk=1)
+        return jnp.concatenate([jnp.where(upper, other, x), jnp.where(upper, x, other)], axis=-1)
 
     def turned(x):
         return jnp.transpose(x[0], (1, 0, 2))
@@ -297,60 +307,74 @@
 
     same = jnp.stack([swap(half_bf, blk=d) for d in others])
     cross = jnp.stack([swap(mapped_bf, sub=1, blk=d) for d in (0,) + tuple(others)])
-    coarse, value, own, own_bf, pack = call(
+    cross, to_sibling, to_far = lax.optimization_barrier((cross, to_sibling, to_far))
+    coarse, value, own, own_bf, share = call(
         pair_kernel,
         (shape(half_shape, F32),) * 3
-        + (shape(half_shape, BF), shape((width, loads // 2 + width), BF)),
+        + (shape(half_shape, BF),) * 2,
         [VMEM] * 5,
         3 * small,
         8 * width * width,
+        limit=4,
     )(keep, got, same, cross, maps)
-    to_sibling, to_far = after(to_sibling, own_bf), after(to_far, own_bf)
-    from_sibling = swap(to_sibling, sub=1)
+    offer = call(
+        offer_kernel,
+        shape(to_sibling.shape, BF),
+        [VMEM] * 4,
+        3 * 10**9,
+        0,
+    )(joined(share), to_sibling, near_fix, maps)
+    from_sibling = swap(offer, sub=1)
     from_others = jnp.stack([swap(to_far, blk=d) for d in others])
-    pack = swap(pack, sub=1)
     values = [value]
     for level in range(2, levels):
         value, own, own_bf = call(
             functools.partial(level_kernel, level),
             (shape(half_shape, F32),) * 2 + (shape(half_shape, BF),),
             [VMEM] * 3,
-            small,
+            2*10**9,
             4 * width * width,
+            limit=4,
         )(own, swap(own_bf, sub=2 ** (level - 1)), maps)
         values.append(value)
     fields = call(
         down_kernel,
         shape((2,) + half_shape, BF),
-        [VMEM] * (6 + len(values)),
+        [VMEM] * (5 + len(values)),
         (levels + 3) * small,
         4 * (levels + 2) * width * width,
-    )(own, swap(own_bf, sub=subs // 2), pack, maps, root_inv, coarse, *values)
-    far_id = jnp.where(even, 0, per - 1)
-    matrix = lax.dynamic_index_in_dim(stiffness[0], after(far_id, own_bf), 0, False)
-    fields, from_sibling, from_others, matrix = lax.optimization_barrier(
-        (fields, from_sibling, from_others, matrix)
-    )
-    across = swap(fields, blk=1)
-    fields = jnp.concatenate(
-        [jnp.where(upper, across, fields), jnp.where(upper, fields, across)], axis=2
-    )
+        limit=4,
+    )(own, swap(own_bf, sub=subs // 2), maps, root_inv, coarse, *values)
+    picked = call(
+        pick_kernel,
+        shape((block, block), BF),
+        [SMEM, VMEM],
+        2 * 10**9,
+        0,
+    )(after(flags, own_bf), turned(dirichlet_inv))
+    fields, from_sibling, from_others, picked = lax.optimization_barrier(
+        (fields, from_sibling, from_others, picked)
+    )
+    fields = joined(fields)
 
     count = 2 + len(others)
-    near, far, near_bf, mine_bf = call(
+    near, far, near_bf, far_bf, mine_bf = call(
         face_kernel,
         (shape((block, loads), F32),) * 2
-        + (shape((block, loads), BF), shape((count, block, loads), BF)),
+        + (shape((block, loads), BF),) * 2
+        + (shape((count, block, loads), BF),),
         [SMEM] + [VMEM] * 7,
         2 * (count + 1) * block * width * loads,
-        count * block * loads * 8,
+        block * loads * 16,
     )(flags, fields, to_sibling, to_far, from_sibling, from_others, near_fix, far_fix)
-
     late = jnp.stack([swap(near_bf, blk=d) for d in others])
+
     core = swap(mine_bf, blk=1)
+    far_id = jnp.where(even, 0, per - 1)
+    matrix = lax.dynamic_index_in_dim(stiffness[0], after(far_id, core), 0, False)
     far_in = go(
-        after(mine_bf[0], core),
-        target=lambda s, b: (s - 1 if s % 2 == 0 else s + 1, b),
+        far_bf,
+        target=lambda s, b: (s, b ^ 1) if s in (0, subs - 1) else (s - 1 if s % 2 == 0 else s + 1, b),
     )
     columns = pattern[0, far_id]
     offset = (columns // per) ^ mine
@@ -363,15 +387,15 @@
     )
     first = 2 * count
     more = 2 * len(others)
-    lists = pltpu.SMEM((2, -(-coupled // 4) * 4), jnp.int32)
-    total, picked = call(
+    lists = pltpu.SMEM((2, -(-coupled // 8) * 8), jnp.int32)
+    total = call(
         couple_kernel,
-        (shape((block, loads), F32), shape((block, block), BF)),
-        [SMEM, SMEM] + [VMEM] * 4,
-        large,
+        shape((block, loads), F32),
+        [SMEM, SMEM] + [VMEM] * 3,
+        10**6,
         2 * coupled * block * block,
         [pltpu.VMEM((first + 1, block, loads), BF), lists],
-    )(slots, flags, matrix, turned(dirichlet_inv), mine_bf, core)
+    )(slots, flags, matrix, mine_bf, core)
     late, total = lax.optimization_barrier((late, total))
     late_core = swap(late, blk=1)
     result = call(

time: 46 us -> 43.6 us (0.948); the launches traced: 45.2 us -> 43.6 us
  local copies, waits for them, and re-layouts: 7.85 us -> 5.83 us
  Pallas kernels: 14 us -> 14.7 us
  starting transfers between devices: 14.2 us -> 13.6 us
    unnamed x16 -> x10, local copies, waits for them, and re-layouts: 4.05 us -> 2.04 us
    pallas_call x2 -> x4, Pallas kernels: 4.37 us -> 5.26 us  [the longest x1 2.54 us: shards(): call(couple_kernel, shape((block, loads), F32), [SMEM, SMEM] + [VMEM] * 3...]
    ppermute x14, starting transfers between devices: 14.2 us -> 13.6 us  [route(): return lax.ppermute(x, ('sub', 'blk'), pairs)]
    pallas_call x1, Pallas kernels: 1.15 us -> 0.59 us  [shards(): call(pair_kernel, (shape(half_shape, F32),) * 3 + (shape(half_shape, BF),...]
  transfers between devices with their start and end apart: 14 -> 14, of which waited for: 8 -> 9; matrix products, arithmetic and copies ran while one was open for 9% -> 9% of each run, Pallas kernels for 15% -> 18%
where the time goes in v4:
time: 43.6 us
  Pallas kernels  14.7 us (34%)
  starting transfers between devices  13.6 us (31%)
  waiting for transfers between devices  9.12 us (21%)
  local copies, waits for them, and re-layouts  5.83 us (13%)
    ppermute x14, starting transfers between devices, route(): return lax.ppermute(x, ('sub', 'blk'), pairs)  13.6 us
    ppermute x14, waiting for transfers between devices, route(): return lax.ppermute(x, ('sub', 'blk'), pairs)  9.12 us
    dynamic_slice x2, local copies, waits for them, and re-layouts, shards(): lax.dynamic_index_in_dim(stiffness[0], after(far_id, core), 0, False)  3.79 us
    pallas_call x1, Pallas kernels, shards(): call(lambda slots_ref, flags_ref, *refs: finish_kernel(slots_ref, flags_r...  3.03 us
    pallas_call x1, Pallas kernels, shards(): call(couple_kernel, shape((block, loads), F32), [SMEM, SMEM] + [VMEM] * 3...  2.54 us
    pallas_call x1, Pallas kernels, shards(): call(start_kernel, tuple((shape(x.shape, x.dtype) for x in given)) + (sha...  2.39 us
    pallas_call x1, Pallas kernels, shards(): call(local_kernel, (shape((block, loads), F32),) * 2 + (shape((block, loa...  2.24 us
    unnamed x10, local copies, waits for them, and re-layouts  2.04 us
  transfers between devices with their start and end apart: 14, of which 9 were waited for; matrix products, arithmetic and copies ran while one was open for 9% of the time, Pallas kernels for 18%

profile of v4, /device:TPU:0, one launch (start us, length us, event | category | flops | bytes accessed | tf_op | source)
XLA Modules:
  0.0 43.6 jit_solution(14032496272898658916)
XLA Ops:
  0.1 1.0 %copy-done = bf16[1,2,375,192]{2,3,1,0:T(8,128)(2,1)S(1)} copy-done((bf16[1,2,375,192]{2,3,1,0:T(8,128)(2,1)S(1)}, bf16[1,2,375,192]{2,3,1,0:T(8,128)(2,1)}, u32[]{:S(2)}) %copy-start) | copy-done | bytes 288024
  1.0 2.4 %shard_map.82 = (bf16[2,192,375]{2,1,0:T(8,128)(2,1)S(1)}, f32[3,192,192]{2,1,0:T(8,128)S(1)}, bf16[2,375,256]{2,1,0:T(8,128)(2,1)S(1)}, f32[2,192,128]{2,1,0:T(8,128)S(1)}, f32[2,192,128]{2,1,0:T(8,128)S(1)}) custom-call(s32[3]{0:T(128)S(1)} %add_convert_fusion.flags_ref, f32[375,2,2,128]{3,2,1,0:T(2,128)} %bitcast.53, bf16[2,192,375]{2,1,0:T(8,128)(2,1)S(1)} %bitcast.47, ...), custom_call_target="tpu_custom_call" | custom-call | flops 73728000 | tf_op jit(solution)/shard_map/pallas_call | solution.py:284
  4.0 1.1 %collective-permute-done.got_ref = f32[2,192,128]{2,1,0:T(8,128)S(1)} collective-permute-done((f32[2,192,128]{2,1,0:T(8,128)S(1)}, f32[2,192,128]{2,1,0:T(8,128)S(1)}, u32[]{:S(2)}, u32[]{:S(2)}) %collective-permute-start) | collective-permute-done | bytes 196640 | tf_op jit(solution)/shard_map/ppermute | solution.py:24
  5.1 3.9 %collective-permute-start.3 = (bf16[192,128]{1,0:T(8,128)(2,1)S(1)}, bf16[192,128]{1,0:T(8,128)(2,1)S(1)}, u32[]{:S(2)}, u32[]{:S(2)}) collective-permute-start(bf16[192,128]{1,0:T(8,128)(2,1)S(1)} %get-tuple-element.73), channel_id=1, source_target_pairs={{0,6},{1,7},{2,4},{3,5},{4,2},{5,3},{6,0},{7,1},{8,14},{9,15},{10,... | collective-permute-start | bytes 147464 | tf_op jit(solution)/shard_map/ppermute | solution.py:24
  9.6 1.1 %copy-done.2 = bf16[1,2,375,375]{3,1,2,0:T(2,128)(2,1)S(1)} copy-done((bf16[1,2,375,375]{3,1,2,0:T(2,128)(2,1)S(1)}, bf16[1,2,375,375]{3,1,2,0:T(2,128)(2,1)}, u32[]{:S(2)}) %copy-start.2) | copy-done | bytes 562524
  10.6 2.2 %shard_map.83 = (f32[375,256]{1,0:T(8,128)S(1)}, f32[375,256]{1,0:T(8,128)S(1)}, bf16[375,448]{1,0:T(8,128)(2,1)S(1)}, bf16[375,448]{1,0:T(8,128)(2,1)S(1)}) custom-call(s32[3]{0:T(128)S(1)} %add_convert_fusion.flags_ref, bf16[2,375,256]{2,1,0:T(8,128)(2,1)S(1)} %get-tuple-element.42.scaled_ref, bf16[375,2,375]{2,1,0:T(2,128)(2,1)S(1)} %bitcast.51, ...), custom_call_target="tpu_custom_call" | custom-call | flops 99999997952 | tf_op jit(solution)/shard_map/pallas_call | solution.py:297
  14.2 1.6 %collective-permute-start.4 = (bf16[192,128]{1,0:T(8,128)(2,1)S(1)}, bf16[192,128]{1,0:T(8,128)(2,1)S(1)}, u32[]{:S(2)}, u32[]{:S(2)}) collective-permute-start(bf16[192,128]{1,0:T(8,128)(2,1)S(1)} %get-tuple-element.49), channel_id=1, source_target_pairs={{0,8},{1,9},{2,10},{3,11},{4,12},{5,13},{6,14},{7,15},{8,0},{9,1},... | collective-permute-start | bytes 147464 | tf_op jit(solution)/shard_map/ppermute | solution.py:24
  15.9 1.3 %collective-permute-start.8 = (bf16[375,448]{1,0:T(8,128)(2,1)S(1)}, bf16[375,448]{1,0:T(8,128)(2,1)S(1)}, u32[]{:S(2)}, u32[]{:S(2)}) collective-permute-start(bf16[375,448]{1,0:T(8,128)(2,1)S(1)} %get-tuple-element.58.far_ref), channel_id=1, source_target_pairs={{0,2},{1,3},{2,0},{3,1},{4,6},{5,7},{6,4},{7,5},{8,10},{9,11},{10,... | collective-permute-start | bytes 1008008 | tf_op jit(solution)/shard_map/ppermute | solution.py:24
  17.6 1.6 %collective-permute-start.7 = (bf16[375,448]{1,0:T(8,128)(2,1)S(1)}, bf16[375,448]{1,0:T(8,128)(2,1)S(1)}, u32[]{:S(2)}, u32[]{:S(2)}) collective-permute-start(bf16[375,448]{1,0:T(8,128)(2,1)S(1)} %shard_map.87), channel_id=1, source_target_pairs={{0,4},{1,5},{2,6},{3,7},{4,0},{5,1},{6,2},{7,3},{8,12},{9,13},{10,... | collective-permute-start | bytes 1008008 | tf_op jit(solution)/shard_map/ppermute | solution.py:24
  19.4 2.7 %collective-permute-start.5 = (bf16[192,128]{1,0:T(8,128)(2,1)S(1)}, bf16[192,128]{1,0:T(8,128)(2,1)S(1)}, u32[]{:S(2)}, u32[]{:S(2)}) collective-permute-start(bf16[192,128]{1,0:T(8,128)(2,1)S(1)} %get-tuple-element.51), channel_id=1, source_target_pairs={{0,16},{1,17},{2,18},{3,19},{4,20},{5,21},{6,22},{7,23},{8,24},{9,... | collective-permute-start | bytes 147464 | tf_op jit(solution)/shard_map/ppermute | solution.py:24
  22.1 1.4 %shard_map.88.refs_1_ = bf16[375,375]{1,0:T(8,128)(2,1)S(1)} custom-call(s32[3]{0:T(128)S(1)} %add_convert_fusion.flags_ref, bf16[375,2,375]{2,1,0:T(2,128)(2,1)S(1)} %bitcast.52), custom_call_target="tpu_custom_call" | custom-call | flops 2000000000 | tf_op jit(solution)/shard_map/pallas_call | solution.py:348
  23.4 1.5 %collective-permute-done.5.got_ref = bf16[192,128]{1,0:T(8,128)(2,1)S(1)} collective-permute-done((bf16[192,128]{1,0:T(8,128)(2,1)S(1)}, bf16[192,128]{1,0:T(8,128)(2,1)S(1)}, u32[]{:S(2)}, u32[]{:S(2)}) %collective-permute-start.5) | collective-permute-done | bytes 49184 | tf_op jit(solution)/shard_map/ppermute | solution.py:24
  25.0 1.0 %shard_map.86 = bf16[2,192,128]{2,1,0:T(8,128)(2,1)S(1)} custom-call(f32[192,128]{1,0:T(8,128)S(1)} %get-tuple-element.50.own_ref, bf16[192,128]{1,0:T(8,128)(2,1)S(1)} %collective-permute-done.5.got_ref, f32[3,192,192]{2,1,0:T(8,128)S(1)} %get-tuple-element.47.map_ref, f32[192,192]{1,0:T(8,128)S(1)} %copy-done.1, ...), custom_call_target="tpu_custom_call" | custom-call | flops 56623104 | bytes 737280 | tf_op jit(solution)/shard_map/pallas_call | solution.py:340
  26.0 0.8 %collective-permute-done.8 = bf16[375,448]{1,0:T(8,128)(2,1)S(1)} collective-permute-done((bf16[375,448]{1,0:T(8,128)(2,1)S(1)}, bf16[375,448]{1,0:T(8,128)(2,1)S(1)}, u32[]{:S(2)}, u32[]{:S(2)}) %collective-permute-start.8) | collective-permute-done | bytes 336032 | tf_op jit(solution)/shard_map/ppermute | solution.py:24
  26.9 1.5 %collective-permute-done.7.near_in_ref = bf16[375,448]{1,0:T(8,128)(2,1)S(1)} collective-permute-done((bf16[375,448]{1,0:T(8,128)(2,1)S(1)}, bf16[375,448]{1,0:T(8,128)(2,1)S(1)}, u32[]{:S(2)}, u32[]{:S(2)}) %collective-permute-start.7) | collective-permute-done | bytes 336032 | tf_op jit(solution)/shard_map/ppermute | solution.py:24
  28.4 1.3 %collective-permute-done.9 = bf16[2,192,128]{2,1,0:T(8,128)(2,1)S(1)} collective-permute-done((bf16[2,192,128]{2,1,0:T(8,128)(2,1)S(1)}, bf16[2,192,128]{2,1,0:T(8,128)(2,1)S(1)}, u32[]{:S(2)}, u32[]{:S(2)}) %collective-permute-start.9) | collective-permute-done | bytes 98336 | tf_op jit(solution)/shard_map/ppermute | solution.py:24
  29.7 0.9 %shard_map.89 = (f32[375,256]{1,0:T(8,128)S(1)}, f32[375,256]{1,0:T(8,128)S(1)}, bf16[375,256]{1,0:T(8,128)(2,1)S(1)}, bf16[375,256]{1,0:T(8,128)(2,1)S(1)}, bf16[3,375,256]{2,1,0:T(8,128)(2,1)S(1)}) custom-call(s32[3]{0:T(128)S(1)} %add_convert_fusion.flags_ref, bf16[2,192,256]{2,1,0:T(8,128)(2,1)S(1)} %pad_maximum_fusion.fields_ref, ...), custom_call_target="tpu_custom_call" | custom-call | flops 147456000 | bytes 1536000 | tf_op jit(solution)/shard_map/pallas_call | solution.py:361
  30.9 0.8 %collective-permute-start.11 = (bf16[375,256]{1,0:T(8,128)(2,1)S(1)}, bf16[375,256]{1,0:T(8,128)(2,1)S(1)}, u32[]{:S(2)}, u32[]{:S(2)}) collective-permute-start(bf16[375,256]{1,0:T(8,128)(2,1)S(1)} %get-tuple-element.67), channel_id=1, source_target_pairs={{0,2},{1,3},{2,0},{3,1},{4,6},{5,7},{6,4},{7,5},{8,10},{9,11},{10,... | collective-permute-start | bytes 576008 | tf_op jit(solution)/shard_map/ppermute | solution.py:24
  31.7 0.9 %collective-permute-done.10.core_ref = bf16[3,375,256]{2,1,0:T(8,128)(2,1)S(1)} collective-permute-done((bf16[3,375,256]{2,1,0:T(8,128)(2,1)S(1)}, bf16[3,375,256]{2,1,0:T(8,128)(2,1)S(1)}, u32[]{:S(2)}, u32[]{:S(2)}) %collective-permute-start.10) | collective-permute-done | bytes 576032 | tf_op jit(solution)/shard_map/ppermute | solution.py:24
  32.7 2.8 %constant_dynamic-slice_fusion = bf16[1,1,16,375,375]{4,2,3,1,0:T(8,128)(2,1)S(1)} fusion(bf16[1,2,16,375,375]{4,2,3,1,0:T(8,128)(2,1)} %param.9, s32[]{:T(128)S(6)} %select_n.91), kind=kLoop, calls=%fused_computation.30 | loop fusion | bytes 9000004 | tf_op jit(solution)/shard_map/jit(dynamic_index_in_dim)/dynamic_slice | solution.py:374
  35.4 1.0 %copy.11 = bf16[1,1,16,375,375]{4,3,2,1,0:T(8,128)(2,1)S(1)} copy(bf16[1,1,16,375,375]{4,2,3,1,0:T(8,128)(2,1)S(1)} %constant_dynamic-slice_fusion) | data formatting | bytes 9000000 | tf_op jit(solution)/shard_map/jit(dynamic_index_in_dim)/dynamic_slice | solution.py:374
  36.5 2.5 %shard_map.90.refs_2_ = f32[375,256]{1,0:T(8,128)S(1)} custom-call(s32[16]{0:T(128)S(1)} %and_select_fusion.1.slots_ref, s32[3]{0:T(128)S(1)} %add_convert_fusion.flags_ref, bf16[16,375,375]{2,1,0:T(8,128)(2,1)S(1)} %bitcast.44, bf16[3,375,256]{2,1,0:T(8,128)(2,1)S(1)} %get-tuple-element.64.mine_ref, bf16[3,375,256]{2,1,0:T(8,128)(2,1)S(1)} %collective-permute-done.10.core_ref), custom_call_target="tpu_custom_call" | custom-call | flops 1000000 | bytes 4500000 | tf_op jit(solution)/shard_map/pallas_call | solution.py:391
  39.2 1.3 %collective-permute-done.12.refs_4_ = bf16[1,375,256]{2,1,0:T(8,128)(2,1)S(1)} collective-permute-done((bf16[1,375,256]{2,1,0:T(8,128)(2,1)S(1)}, bf16[1,375,256]{2,1,0:T(8,128)(2,1)S(1)}, u32[]{:S(2)}, u32[]{:S(2)}) %collective-permute-start.12) | collective-permute-done | bytes 192032 | tf_op jit(solution)/shard_map/ppermute | solution.py:24
  40.5 3.0 %shard_map.91 = f32[375,2,2,128]{3,2,1,0:T(2,128)} custom-call(s32[16]{0:T(128)S(1)} %and_select_fusion.1.slots_ref, s32[3]{0:T(128)S(1)} %add_convert_fusion.flags_ref, bf16[16,375,375]{2,1,0:T(8,128)(2,1)S(1)} %bitcast.45, bf16[375,375]{1,0:T(8,128)(2,1)S(1)} %shard_map.88.refs_1_, f32[375,256]{1,0:T(8,128)S(1)} %shard_map.90.refs_2_, ...), custom_call_target="tpu_custom_call" | custom-call | flops 72000000 | bytes 1536000 | tf_op jit(solution)/shard_map/pallas_call | solution.py:401
  (34 shorter events, 3.8 us)
Async XLA Ops:
  0.1 1.0 %copy-start = (bf16[1,2,375,192]{2,3,1,0:T(8,128)(2,1)S(1)}, bf16[1,2,375,192]{2,3,1,0:T(8,128)(2,1)}, u32[]{:S(2)}) copy-start(bf16[1,2,375,192]{2,3,1,0:T(8,128)(2,1)} %param.13) | copy-start | bytes 864004
  3.4 1.6 %collective-permute-start = (f32[2,192,128]{2,1,0:T(8,128)S(1)}, f32[2,192,128]{2,1,0:T(8,128)S(1)}, u32[]{:S(2)}, u32[]{:S(2)}) collective-permute-start(f32[2,192,128]{2,1,0:T(8,128)S(1)} %get-tuple-element.40), channel_id=1, source_target_pairs={{0,1},{1,0},{2,3},{3,2},{4,5},{5,4},{6,7},{7,6},{8,9},{9,8},{10,11... | collective-permute-start | bytes 589832 | tf_op jit(solution)/shard_map/ppermute | solution.py:24
  5.1 7.8 %collective-permute-start.3 = (bf16[192,128]{1,0:T(8,128)(2,1)S(1)}, bf16[192,128]{1,0:T(8,128)(2,1)S(1)}, u32[]{:S(2)}, u32[]{:S(2)}) collective-permute-start(bf16[192,128]{1,0:T(8,128)(2,1)S(1)} %get-tuple-element.73), channel_id=1, source_target_pairs={{0,6},{1,7},{2,4},{3,5},{4,2},{5,3},{6,0},{7,1},{8,14},{9,15},{10,... | collective-permute-start | bytes 147464 | tf_op jit(solution)/shard_map/ppermute | solution.py:24
  8.9 4.1 %collective-permute-start.2 = (bf16[192,128]{1,0:T(8,128)(2,1)S(1)}, bf16[192,128]{1,0:T(8,128)(2,1)S(1)}, u32[]{:S(2)}, u32[]{:S(2)}) collective-permute-start(bf16[192,128]{1,0:T(8,128)(2,1)S(1)} %get-tuple-element.73), channel_id=1, source_target_pairs={{0,4},{1,5},{2,6},{3,7},{4,0},{5,1},{6,2},{7,3},{8,12},{9,13},{10,... | collective-permute-start | bytes 147464 | tf_op jit(solution)/shard_map/ppermute | solution.py:24
  9.5 4.1 %collective-permute-start.1 = (bf16[192,128]{1,0:T(8,128)(2,1)S(1)}, bf16[192,128]{1,0:T(8,128)(2,1)S(1)}, u32[]{:S(2)}, u32[]{:S(2)}) collective-permute-start(bf16[192,128]{1,0:T(8,128)(2,1)S(1)} %get-tuple-element.74), channel_id=1, source_target_pairs={{0,2},{1,3},{2,0},{3,1},{4,6},{5,7},{6,4},{7,5},{8,10},{9,11},{10,... | collective-permute-start | bytes 147464 | tf_op jit(solution)/shard_map/ppermute | solution.py:24
  9.6 1.1 %copy-start.2 = (bf16[1,2,375,375]{3,1,2,0:T(2,128)(2,1)S(1)}, bf16[1,2,375,375]{3,1,2,0:T(2,128)(2,1)}, u32[]{:S(2)}) copy-start(bf16[1,2,375,375]{3,1,2,0:T(2,128)(2,1)} %param.11) | copy-start | bytes 1687504
  14.2 3.0 %collective-permute-start.6 = (bf16[192,128]{1,0:T(8,128)(2,1)S(1)}, bf16[192,128]{1,0:T(8,128)(2,1)S(1)}, u32[]{:S(2)}, u32[]{:S(2)}) collective-permute-start(bf16[192,128]{1,0:T(8,128)(2,1)S(1)} %get-tuple-element.55), channel_id=1, source_target_pairs={{0,1},{1,0},{2,3},{3,2},{4,5},{5,4},{6,7},{7,6},{8,9},{9,8},{10,11... | collective-permute-start | bytes 147464 | tf_op jit(solution)/shard_map/ppermute | solution.py:24
  14.2 4.9 %collective-permute-start.4 = (bf16[192,128]{1,0:T(8,128)(2,1)S(1)}, bf16[192,128]{1,0:T(8,128)(2,1)S(1)}, u32[]{:S(2)}, u32[]{:S(2)}) collective-permute-start(bf16[192,128]{1,0:T(8,128)(2,1)S(1)} %get-tuple-element.49), channel_id=1, source_target_pairs={{0,8},{1,9},{2,10},{3,11},{4,12},{5,13},{6,14},{7,15},{8,0},{9,1},... | collective-permute-start | bytes 147464 | tf_op jit(solution)/shard_map/ppermute | solution.py:24
  15.9 11.0 %collective-permute-start.8 = (bf16[375,448]{1,0:T(8,128)(2,1)S(1)}, bf16[375,448]{1,0:T(8,128)(2,1)S(1)}, u32[]{:S(2)}, u32[]{:S(2)}) collective-permute-start(bf16[375,448]{1,0:T(8,128)(2,1)S(1)} %get-tuple-element.58.far_ref), channel_id=1, source_target_pairs={{0,2},{1,3},{2,0},{3,1},{4,6},{5,7},{6,4},{7,5},{8,10},{9,11},{10,... | collective-permute-start | bytes 1008008 | tf_op jit(solution)/shard_map/ppermute | solution.py:24
  17.5 4.5 %copy-start.3 = (bf16[1,2,375,375]{3,1,2,0:T(2,128)(2,1)S(1)}, bf16[1,2,375,375]{3,1,2,0:T(2,128)(2,1)}, u32[]{:S(2)}) copy-start(bf16[1,2,375,375]{3,1,2,0:T(2,128)(2,1)} %param.12) | copy-start | bytes 1687504
  17.6 10.8 %collective-permute-start.7 = (bf16[375,448]{1,0:T(8,128)(2,1)S(1)}, bf16[375,448]{1,0:T(8,128)(2,1)S(1)}, u32[]{:S(2)}, u32[]{:S(2)}) collective-permute-start(bf16[375,448]{1,0:T(8,128)(2,1)S(1)} %shard_map.87), channel_id=1, source_target_pairs={{0,4},{1,5},{2,6},{3,7},{4,0},{5,1},{6,2},{7,3},{8,12},{9,13},{10,... | collective-permute-start | bytes 1008008 | tf_op jit(solution)/shard_map/ppermute | solution.py:24
  19.4 5.6 %copy-start.1 = (f32[192,192]{1,0:T(8,128)S(1)}, f32[192,192]{1,0:T(8,128)}, u32[]{:S(2)}) copy-start(f32[192,192]{1,0:T(8,128)} %root_ref.1) | copy-start | bytes 442372
  19.4 5.6 %collective-permute-start.5 = (bf16[192,128]{1,0:T(8,128)(2,1)S(1)}, bf16[192,128]{1,0:T(8,128)(2,1)S(1)}, u32[]{:S(2)}, u32[]{:S(2)}) collective-permute-start(bf16[192,128]{1,0:T(8,128)(2,1)S(1)} %get-tuple-element.51), channel_id=1, source_target_pairs={{0,16},{1,17},{2,18},{3,19},{4,20},{5,21},{6,22},{7,23},{8,24},{9,... | collective-permute-start | bytes 147464 | tf_op jit(solution)/shard_map/ppermute | solution.py:24
  22.1 8.8 %copy-start.4 = (s32[1,2,16]{2,1,0:T(2,128)S(1)}, s32[1,2,16]{2,1,0:T(2,128)}, u32[]{:S(2)}) copy-start(s32[1,2,16]{2,1,0:T(2,128)} %param.10) | copy-start | bytes 388
  28.4 1.3 %collective-permute-start.9 = (bf16[2,192,128]{2,1,0:T(8,128)(2,1)S(1)}, bf16[2,192,128]{2,1,0:T(8,128)(2,1)S(1)}, u32[]{:S(2)}, u32[]{:S(2)}) collective-permute-start(bf16[2,192,128]{2,1,0:T(8,128)(2,1)S(1)} %shard_map.86), channel_id=1, source_target_pairs={{0,1},{1,0},{2,3},{3,2},{4,5},{5,4},{6,7},{7,6},{8,9},{9,8},{10,11... | collective-permute-start | bytes 294920 | tf_op jit(solution)/shard_map/ppermute | solution.py:24
  30.6 2.1 %collective-permute-start.10 = (bf16[3,375,256]{2,1,0:T(8,128)(2,1)S(1)}, bf16[3,375,256]{2,1,0:T(8,128)(2,1)S(1)}, u32[]{:S(2)}, u32[]{:S(2)}) collective-permute-start(bf16[3,375,256]{2,1,0:T(8,128)(2,1)S(1)} %get-tuple-element.64.mine_ref), channel_id=1, source_target_pairs={{0,1},{1,0},{2,3},{3,2},{4,5},{5,4},{6,7},{7,6},{8,9},{9,8},{10,11... | collective-permute-start | bytes 1728008 | tf_op jit(solution)/shard_map/ppermute | solution.py:24
  30.9 8.2 %collective-permute-start.11 = (bf16[375,256]{1,0:T(8,128)(2,1)S(1)}, bf16[375,256]{1,0:T(8,128)(2,1)S(1)}, u32[]{:S(2)}, u32[]{:S(2)}) collective-permute-start(bf16[375,256]{1,0:T(8,128)(2,1)S(1)} %get-tuple-element.67), channel_id=1, source_target_pairs={{0,2},{1,3},{2,0},{3,1},{4,6},{5,7},{6,4},{7,5},{8,10},{9,11},{10,... | collective-permute-start | bytes 576008 | tf_op jit(solution)/shard_map/ppermute | solution.py:24
  31.7 7.6 %collective-permute-start.13 = (bf16[375,256]{1,0:T(8,128)(2,1)S(1)}, bf16[375,256]{1,0:T(8,128)(2,1)S(1)}, u32[]{:S(2)}, u32[]{:S(2)}) collective-permute-start(bf16[375,256]{1,0:T(8,128)(2,1)S(1)} %get-tuple-element.71), channel_id=1, source_target_pairs={{0,1},{1,0},{2,3},{3,2},{4,8},{5,9},{6,10},{7,11},{8,4},{9,5},{10,... | collective-permute-start | bytes 576008 | tf_op jit(solution)/shard_map/ppermute | solution.py:24
  39.0 1.5 %collective-permute-start.12 = (bf16[1,375,256]{2,1,0:T(8,128)(2,1)S(1)}, bf16[1,375,256]{2,1,0:T(8,128)(2,1)S(1)}, u32[]{:S(2)}, u32[]{:S(2)}) collective-permute-start(bf16[1,375,256]{2,1,0:T(8,128)(2,1)S(1)} %bitcast.48), channel_id=1, source_target_pairs={{0,1},{1,0},{2,3},{3,2},{4,5},{5,4},{6,7},{7,6},{8,9},{9,8},{10,11... | collective-permute-start | bytes 576008 | tf_op jit(solution)/shard_map/ppermute | solution.py:24
